TPU v7x, 32 devices: a whole 2x2x4 slice. The times are simulated.
32 devices in a mesh: node: 8 (over z, x), feat: 4 (over y, core).
Axes of the slice: x: 2, y: 2, z: 4, core: 2. Of those that a mesh axis runs over, the one named last changes fastest.
Arguments:
- features: float32 [6144, 1024], P('node', 'feat'), may hold values from -6 to 6
- degrees: int32 [6144], P('node'), may hold values from 1 to 4
- tile_row: int32 [8, 33], P('node'), may hold values from 0 to 5, as said below
- tile_col: int32 [8, 33], P('node'), may hold values from 0 to 13, as said below
- tile_count: int32 [8], P('node'), may hold values from 19 to 33, as said below
- send_block: int32 [8, 8], replicated, may hold values from 0 to 5
- tile_val: bfloat16 [8, 33, 128, 128], P('node'), may hold values from -0.15625 to 0.15625
- weight: bfloat16 [1024, 3, 1024], P('node', None, 'feat'), may hold values from -0.109375 to 0.109375
- out_bias: float32 [1024], replicated, may hold values from -3 to 3
- cotangent: bfloat16 [6144, 1024], P(('node', 'feat')), may hold values from -0.076171875 to 0.076171875
Outputs:
- output: bfloat16 [6144, 1024], P(('node', 'feat'))
- weight_grad: float32 [1024, 3, 1024], P('node', None, 'feat')
- bias_grad: float32 [1024], replicated
Inputs may be any that keep to these rules, and one draw needn't show every extreme that they name: `tile_row`: the row block of each slot; for each other part q, between 1 and 3 live tiles of part p read slot 6 + q, each at a different row block. `tile_col`: below 6: the part's own row block; 6 + q: the block that part q sends; the first 12 slots of each part read own blocks, tile i < 6 at row block i, column i; slots past tile_count read 0; no tile reads slot 6 + p in part p. `tile_count`: live tiles come first in each part; some part has 33 live tiles.
All inputs are finite; a program needn't handle non-finite values.
Results may differ from a plain program's by a relative error of at most 0.0057.
Values may be sent and summed in bfloat16 or wider, within the bound.
A program may use at most 192 MiB of HBM per device.

v0:
```python
import jax
import jax.numpy as jnp
from jax import lax
from jax.sharding import PartitionSpec as P

HOPS = 2


def propagate(source, tile_rows, tile_cols, tile_values, is_live, send_row):
    block_size = tile_values.shape[-1]
    panel_width = source.shape[1]
    own_blocks = source.reshape(-1, block_size, panel_width)
    outgoing = own_blocks[send_row]
    arrived = lax.all_to_all(outgoing, "node", split_axis=0, concat_axis=0, tiled=True)
    frame = jnp.concatenate([own_blocks, arrived], axis=0)
    sources = frame[tile_cols]
    product = jnp.einsum("tij,tjc->tic", tile_values, sources, preferred_element_type=jnp.float32)
    block_ids = jnp.arange(own_blocks.shape[0], dtype=jnp.int32)
    onehot = ((tile_rows[:, None] == block_ids[None, :]) & is_live[:, None]).astype(jnp.float32)
    summed = jnp.einsum("tr,tic->ric", onehot, product, precision=lax.Precision.HIGHEST)
    return summed.reshape(source.shape[0], panel_width)


def local(
    features,
    degrees,
    tile_row,
    tile_col,
    tile_count,
    send_block,
    tile_val,
    weight,
    out_bias,
    cotangent,
):
    node_index = lax.axis_index("node")
    send_row = lax.dynamic_index_in_dim(send_block, node_index, 0, keepdims=False)
    tile_rows = tile_row[0]
    tile_cols = tile_col[0]
    tile_values = tile_val[0]
    is_live = jnp.arange(tile_rows.shape[0], dtype=jnp.int32) < tile_count[0]
    row_scale = lax.rsqrt(degrees.astype(jnp.float32))[:, None]
    source = (features * row_scale).astype(jnp.bfloat16)
    hop_list = [features.astype(jnp.bfloat16)]
    for hop_number in range(HOPS):
        summed = propagate(source, tile_rows, tile_cols, tile_values, is_live, send_row)
        hop_list.append((summed * row_scale).astype(jnp.bfloat16))
        if hop_number + 1 < HOPS:
            source = (summed * row_scale * row_scale).astype(jnp.bfloat16)
    stacked = jnp.stack(hop_list, axis=1)
    hop_total = stacked.shape[1]
    flat_rows = stacked.reshape(stacked.shape[0], -1)
    piece = lax.all_gather(weight, "node", axis=0, tiled=True)
    flat_piece = piece.reshape(piece.shape[0], -1)
    panel_terms = lax.dot_general(
        flat_rows, flat_piece, (((1,), (1,)), ((), ())), preferred_element_type=jnp.float32
    )
    linear = lax.psum_scatter(panel_terms, "feat", scatter_dimension=0, tiled=True)
    linear = linear + out_bias[None, :]
    sigmoid_val = jax.nn.sigmoid(linear)
    output = (linear * sigmoid_val).astype(jnp.bfloat16)
    grad_linear = (
        cotangent.astype(jnp.float32) * sigmoid_val * (1.0 + linear * (1.0 - sigmoid_val))
    ).astype(jnp.bfloat16)
    bias_grad = lax.psum(jnp.sum(grad_linear.astype(jnp.float32), axis=0), ("node", "feat"))
    grad_all = lax.all_gather(grad_linear, "feat", axis=0, tiled=True)
    term = lax.dot_general(
        grad_all, flat_rows, (((0,), (0,)), ((), ())), preferred_element_type=jnp.float32
    )
    weight_grad = lax.psum_scatter(
        term.reshape(weight.shape[0] * lax.axis_size("node"), hop_total, -1),
        "node",
        scatter_dimension=0,
        tiled=True,
    )
    return (output, weight_grad, bias_grad)


def solution(mesh):
    in_specs = (
        P("node", "feat"),
        P("node"),
        P("node", None),
        P("node", None),
        P("node"),
        P(),
        P("node", None, None, None),
        P("node", None, "feat"),
        P(),
        P(("node", "feat"), None),
    )
    out_specs = (P(("node", "feat"), None), P("node", None, "feat"), P())
    return jax.shard_map(local, mesh=mesh, in_specs=in_specs, out_specs=out_specs, check_vma=False)
```

profile of v0, /device:TPU:0, one launch (start us, length us, event | category | flops | bytes accessed | tf_op | source)
XLA Modules:
  0.0 248.6 jit_solution(8604299513341819620)
XLA Ops:
  8.7 2.4 convert_bitcast_fusion
  11.1 1.4 gather_fusion
  12.5 7.3 %all-to-all-start = ((bf16[8,128,256]{2,1,0:T(8,128)(2,1)}), bf16[8,128,256]{2,1,0:T(8,128)(2,1)S(1)}, u32[]{:S(2)}, u32[]{:S(2)}) async-start(bf16[8,128,256]{2,1,0:T(8,128)(2,1)} %gather_fusion), calls=%async_computation | async-start | bytes 1048576 | tf_op jit(solution)/shard_map/all_to_all | solution.py:14
  21.3 12.9 %all-to-all-done = bf16[8,128,256]{2,1,0:T(8,128)(2,1)S(1)} async-done(((bf16[8,128,256]{2,1,0:T(8,128)(2,1)}), bf16[8,128,256]{2,1,0:T(8,128)(2,1)S(1)}, u32[]{:S(2)}, u32[]{:S(2)}) %all-to-all-start) | async-done | bytes 524320 | tf_op jit(solution)/shard_map/all_to_all | solution.py:14
  34.3 2.2 gather_fusion.1
  36.5 4.4 %fusion.9 = f32[33,256,128]{2,1,0:T(8,128)} fusion(bf16[33,128,256]{2,1,0:T(8,128)(2,1)} %gather_fusion.1, bf16[1,33,128,128]{3,2,1,0:T(8,128)(2,1)S(1)} %copy-done), kind=kOutput, calls=%fused_computation.15 | convolution fusion | flops 276824064 | bytes 7569408 | tf_op jit(solution)/shard_map/tij,tjc->tic/dot_general | solution.py:17
  41.0 5.8 %copy.19 = f32[33,256,128]{1,0,2:T(8,128)} copy(f32[33,256,128]{2,1,0:T(8,128)} %fusion.9) | data formatting | bytes 8650752 | tf_op jit(solution)/shard_map/tij,tjc->tic/dot_general | solution.py:17
  46.8 4.3 %multiply_convert_fusion = (bf16[6,128,256]{2,0,1:T(8,128)(2,1)S(1)}, f32[6,128,256]{2,0,1:T(8,128)S(1)}) fusion(f32[6,128]{0,1:T(8,128)S(1)} %copy.14, f32[33,256,128]{1,0,2:T(8,128)} %copy.19, s32[33]{0:T(128)S(1)} %bitcast.60, pred[33]{0:T(512)(128)(4,1)S(1)} %iota_compare_fusion.1), kind=kOutput, calls=%fused_computation.17 | convolution fusion | flops 78446992 | bytes 5508261 | tf_op jit(solution)/shard_map/tr,tic->ric/dot_general | solution.py:20
  51.2 1.4 gather_fusion.2
  52.5 4.1 %all-to-all-start.1 = ((bf16[8,128,256]{2,1,0:T(8,128)(2,1)}), bf16[8,128,256]{2,1,0:T(8,128)(2,1)}, u32[]{:S(2)}, u32[]{:S(2)}) async-start(bf16[8,128,256]{2,1,0:T(8,128)(2,1)} %gather_fusion.2), calls=%async_computation.1 | async-start | bytes 1048576 | tf_op jit(solution)/shard_map/all_to_all | solution.py:14
  56.8 1.1 copy.13
  57.9 19.7 %all-to-all-done.1 = bf16[8,128,256]{2,1,0:T(8,128)(2,1)} async-done(((bf16[8,128,256]{2,1,0:T(8,128)(2,1)}), bf16[8,128,256]{2,1,0:T(8,128)(2,1)}, u32[]{:S(2)}, u32[]{:S(2)}) %all-to-all-start.1) | async-done | bytes 524320 | tf_op jit(solution)/shard_map/all_to_all | solution.py:14
  77.6 1.1 pad_maximum_fusion.2
  78.7 2.2 gather_fusion.3
  81.0 4.4 %fusion.7 = f32[33,256,128]{2,1,0:T(8,128)} fusion(bf16[33,128,256]{2,1,0:T(8,128)(2,1)} %gather_fusion.3, bf16[1,33,128,128]{3,2,1,0:T(8,128)(2,1)S(1)} %copy-done), kind=kOutput, calls=%fused_computation.13 | convolution fusion | flops 276824064 | bytes 7569408 | tf_op jit(solution)/shard_map/tij,tjc->tic/dot_general | solution.py:17
  85.4 5.8 %copy.20 = f32[33,256,128]{1,0,2:T(8,128)} copy(f32[33,256,128]{2,1,0:T(8,128)} %fusion.7) | data formatting | bytes 8650752 | tf_op jit(solution)/shard_map/tij,tjc->tic/dot_general | solution.py:17
  91.2 4.3 %fusion = f32[6,128,256]{2,0,1:T(8,128)S(1)} fusion(f32[33,256,128]{1,0,2:T(8,128)} %copy.20, s32[33]{0:T(128)S(1)} %bitcast.61, pred[33]{0:T(512)(128)(4,1)S(1)} %iota_compare_fusion.1), kind=kOutput, calls=%fused_computation.4 | convolution fusion | flops 77857168 | bytes 5111973 | tf_op jit(solution)/shard_map/tr,tic->ric/dot_general | solution.py:20
  97.6 4.5 %convolution_bitcast_fusion = f32[768,1024]{1,0:T(8,128)} fusion(bf16[1024,3,256]{2,0,1:T(8,128)(2,1)} %all-gather.3.cloned.1.call-done, bf16[768,1,256]{2,0,1:T(8,128)(2,1)S(1)} %get-tuple-element.9, bf16[768,1,256]{2,0,1:T(8,128)(2,1)S(1)} %get-tuple-element.8, bf16[768,1,256]{2,0,1:T(8,128)(2,1)S(1)} %copy-done.2), kind=kOutput, calls=%fused_computation.8 | convolution fusion | flops 1209139200 | bytes 5898240 | tf_op jit(solution)/shard_map/dot_general | solution.py:55
  102.2 36.7 %reduce-scatter.3.cloned.1.call-done = f32[192,1024]{1,0:T(8,128)} async-done(((f32[768,1024]{1,0:T(8,128)}), f32[192,1024]{1,0:T(8,128)}) %reduce-scatter.3.cloned.1.call-update) | async-done | bytes 786448 | tf_op jit(solution)/shard_map/reduce_scatter | solution.py:58
  138.9 2.4 convert_reduce_fusion
  142.4 18.7 %all-gather.5.cloned.1.call-done = bf16[768,1024]{1,0:T(8,128)(2,1)} async-done(((bf16[192,1024]{1,0:T(8,128)(2,1)}), bf16[768,1024]{1,0:T(8,128)(2,1)}) %all-gather.5.cloned.1.call-update) | async-done | bytes 1572880 | tf_op jit(solution)/shard_map/all_gather | solution.py:66
  161.1 4.5 %fusion.4 = f32[1024,3,256]{2,0,1:T(8,128)} fusion(bf16[768,1024]{1,0:T(8,128)(2,1)} %all-gather.5.cloned.1.call-done, bf16[768,3,256]{0,2,1:T(8,128)(2,1)S(1)} %copy.18), kind=kOutput, calls=%fused_computation.9 | convolution fusion | flops 1207959552 | bytes 5898240 | tf_op jit(solution)/shard_map/dot_general | solution.py:67
  165.6 41.2 %psum.7 = f32[1024]{0:T(1024)} all-reduce(f32[1024]{0:T(1024)S(1)} %get-tuple-element.3), channel_id=1, replica_groups=mesh['node'=8,'feat'=4] {'node','feat'}, use_global_device_ids=true, to_apply=%region_3.4 | all-reduce | flops 1024 | bytes 8192 | tf_op jit(solution)/shard_map/psum | solution.py:65
  206.9 35.2 %reduce-scatter.5.cloned.1.call-done = f32[128,3,256]{2,0,1:T(8,128)} async-done(((f32[1024,3,256]{2,0,1:T(8,128)}), f32[128,3,256]{2,0,1:T(8,128)}) %reduce-scatter.5.cloned.1.call-update) | async-done | bytes 393232 | tf_op jit(solution)/shard_map/reduce_scatter | solution.py:70
  (36 shorter events, 5.8 us)
Async XLA Ops:
  7.2 29.4 %copy-start = (bf16[1,33,128,128]{3,2,1,0:T(8,128)(2,1)S(1)}, bf16[1,33,128,128]{3,2,1,0:T(8,128)(2,1)}, u32[]{:S(2)}) copy-start(bf16[1,33,128,128]{3,2,1,0:T(8,128)(2,1)} %param.16) | copy-start | bytes 3244036
  11.1 10.1 %copy-start.6 = (s32[1,33]{1,0:T(1,128)S(1)}, s32[1,33]{1,0:T(1,128)}, u32[]{:S(2)}) copy-start(s32[1,33]{1,0:T(1,128)} %param.13) | copy-start | bytes 400
  12.5 21.7 %all-to-all-start = ((bf16[8,128,256]{2,1,0:T(8,128)(2,1)}), bf16[8,128,256]{2,1,0:T(8,128)(2,1)S(1)}, u32[]{:S(2)}, u32[]{:S(2)}) async-start(bf16[8,128,256]{2,1,0:T(8,128)(2,1)} %gather_fusion), calls=%async_computation | async-start | bytes 1048576 | tf_op jit(solution)/shard_map/all_to_all | solution.py:14
  19.7 77.1 %all-gather.3.cloned.1.call-start = ((), (), s32[]{:S(2)}) async-start(), calls=%async_computation.4 | async-start | bytes 1769472 | tf_op jit(solution)/shard_map/all_gather | solution.py:53
  41.0 5.8 %copy-start.5 = (s32[1,33]{1,0:T(1,128)S(1)}, s32[1,33]{1,0:T(1,128)}, u32[]{:S(2)}) copy-start(s32[1,33]{1,0:T(1,128)} %param.12) | copy-start | bytes 400
  52.5 25.1 %all-to-all-start.1 = ((bf16[8,128,256]{2,1,0:T(8,128)(2,1)}), bf16[8,128,256]{2,1,0:T(8,128)(2,1)}, u32[]{:S(2)}, u32[]{:S(2)}) async-start(bf16[8,128,256]{2,1,0:T(8,128)(2,1)} %gather_fusion.2), calls=%async_computation.1 | async-start | bytes 1048576 | tf_op jit(solution)/shard_map/all_to_all | solution.py:14
  56.7 82.2 %reduce-scatter.3.cloned.1.call-start = ((), (), s32[]{:S(2)}) async-start(), calls=%async_computation.5 | async-start | bytes 3932160 | tf_op jit(solution)/shard_map/reduce_scatter | solution.py:58
  95.5 1.1 copy-start.1
  96.6 1.0 copy-start.2
  102.1 36.8 %copy-start.3 = (bf16[192,1024]{1,0:T(8,128)(2,1)S(1)}, bf16[192,1024]{1,0:T(8,128)(2,1)}, u32[]{:S(2)}) copy-start(bf16[192,1024]{1,0:T(8,128)(2,1)} %param.19) | copy-start | bytes 1179652
  102.1 36.8 %copy-start.4 = (f32[1024]{0:T(1024)S(1)}, f32[1024]{0:T(1024)}, u32[]{:S(2)}) copy-start(f32[1024]{0:T(1024)} %param.18) | copy-start | bytes 12292
  102.1 59.0 %all-gather.5.cloned.1.call-start = ((), (), s32[]{:S(2)}) async-start(), calls=%async_computation.6 | async-start | bytes 1966080 | tf_op jit(solution)/shard_map/all_gather | solution.py:66
  141.3 100.7 %reduce-scatter.5.cloned.1.call-start = ((), (), s32[]{:S(2)}) async-start(), calls=%async_computation.7 | async-start | bytes 3538944 | tf_op jit(solution)/shard_map/reduce_scatter | solution.py:70
Sparse Core Ops, SparseCore 0:
  22.7 54.5 all-gather.2
  102.2 36.5 reduce-scatter.2
  141.4 19.6 all-gather.4
  165.8 76.2 reduce-scatter.4
where the time goes:
time: 249 us
  waiting for transfers between devices  124 us (50%)
  blocking collectives  41.2 us (17%)
  matrix products  26.4 us (11%)
  local copies, waits for them, and re-layouts  22.8 us (9%)
  between operations  14.5 us (6%)
  starting transfers between devices  11.7 us (5%)
  other arithmetic  7.83 us (3%)
    psum x1, blocking collectives, local(): lax.psum(jnp.sum(grad_linear.astype(jnp.float32), axis=0), ('node', 'feat'))  41.2 us
    reduce_scatter x1, waiting for transfers between devices, local(): lax.psum_scatter(panel_terms, 'feat', scatter_dimension=0, tiled=True)  36.7 us
    reduce_scatter x1, waiting for transfers between devices, local(): lax.psum_scatter(term.reshape(weight.shape[0] * lax.axis_size('node'), ho...  35.2 us
    all_to_all x2, waiting for transfers between devices, propagate(): lax.all_to_all(outgoing, 'node', split_axis=0, concat_axis=0, tiled=True)  32.7 us
    all_gather x1, waiting for transfers between devices, local(): grad_all = lax.all_gather(grad_linear, 'feat', axis=0, tiled=True)  18.7 us
    dot_general x2, local copies, waits for them, and re-layouts, propagate(): jnp.einsum('tij,tjc->tic', tile_values, sources, preferred_element_type=j...  11.6 us
    all_to_all x2, starting transfers between devices, propagate(): lax.all_to_all(outgoing, 'node', split_axis=0, concat_axis=0, tiled=True)  11.4 us
    dot_general x2, matrix products, propagate(): jnp.einsum('tij,tjc->tic', tile_values, sources, preferred_element_type=j...  8.88 us
  transfers between devices with their start and end apart: 6, of which 5 were waited for; matrix products, arithmetic and copies ran while one was open for 16% of the time, Pallas kernels for 0%

commit v1 on v0

v1 whole, which is shorter than its diff:
```python
import functools

import jax
import jax.numpy as jnp
from jax import lax
from jax.experimental import pallas as pl
from jax.experimental.pallas import tpu as pltpu
from jax.sharding import PartitionSpec as P

HOPS = 2
PIECES = 2
MESH = pl.DeviceIdType.MESH


def matrix_kernel(tile_row, tile_col, tile_count, tile_val, matrix):
    block = tile_val.shape[-1]
    matrix[...] = jnp.zeros_like(matrix)

    def place(tile, carry):
        row = pl.multiple_of(tile_row[0, tile] * block, block)
        col = pl.multiple_of(tile_col[0, tile] * block, block)
        here = (pl.ds(row, block), pl.ds(col, block))
        total = matrix[here].astype(jnp.float32) + tile_val[0, tile].astype(jnp.float32)
        matrix[here] = total.astype(jnp.bfloat16)
        return carry

    lax.fori_loop(0, tile_count[0], place, 0)


def dense_matrix(tile_row, tile_col, tile_count, tile_val, own_nodes):
    block = tile_val.shape[-1]
    columns = own_nodes + lax.axis_size("node") * block
    smem = pl.BlockSpec(memory_space=pltpu.SMEM)
    vmem = pl.BlockSpec(memory_space=pltpu.VMEM)
    return pl.pallas_call(
        matrix_kernel,
        out_shape=jax.ShapeDtypeStruct((own_nodes, columns), jnp.bfloat16),
        in_specs=[smem, smem, smem, vmem],
        out_specs=vmem,
        compiler_params=pltpu.CompilerParams(vmem_limit_bytes=40 * 1024 * 1024),
        name="matrix",
    )(tile_row, tile_col, tile_count, tile_val)


def hops_kernel(
    nodes, send_block, features, scale, matrix, rows, source, outgoing, frame, acc, s_sem, r_sem
):
    node = lax.axis_index("node")
    feat = lax.axis_index("feat")
    own_nodes, panel = features.shape
    block = frame.shape[2]
    barrier = pltpu.get_barrier_semaphore()
    for hop in range(1, nodes):
        pl.semaphore_signal(
            barrier, inc=1, device_id=(lax.rem(node + hop, nodes), feat), device_id_type=MESH
        )

    def put_source(values):
        source[...] = values.astype(jnp.bfloat16).reshape(source.shape)

    put_source(features[...] * scale[...])
    rows[:, pl.ds(0, panel)] = features[...].astype(jnp.bfloat16)
    pl.semaphore_wait(barrier, nodes - 1)

    group = min(nodes, 8)
    copies = []
    for step in range(HOPS):
        arrivals = []
        for hop in range(1, nodes):
            part = lax.rem(node + hop, nodes)
            outgoing[step, hop - 1] = source[send_block[node, part]]
            copy = pltpu.make_async_remote_copy(
                src_ref=outgoing.at[step, hop - 1],
                dst_ref=frame.at[step, node],
                send_sem=s_sem.at[step, hop - 1],
                recv_sem=r_sem.at[step, hop - 1],
                device_id=(part, feat),
                device_id_type=MESH,
            )
            copy.start()
            copies.append(copy)
            sender = lax.rem(node + nodes - hop, nodes)
            arrivals.append(
                pltpu.make_async_remote_copy(
                    src_ref=outgoing.at[step, hop - 1],
                    dst_ref=frame.at[step, sender],
                    send_sem=s_sem.at[step, hop - 1],
                    recv_sem=r_sem.at[step, hop - 1],
                    device_id=(part, feat),
                    device_id_type=MESH,
                )
            )
        frame[step, node] = jnp.zeros((block, panel), jnp.bfloat16)
        acc[...] = jnp.dot(
            matrix[:, pl.ds(0, own_nodes)],
            source[...].reshape(own_nodes, panel),
            preferred_element_type=jnp.float32,
        )
        for arrival in arrivals:
            arrival.wait_recv()

        def add(first):
            start = pl.multiple_of(own_nodes + first * block, block)
            acc[...] += jnp.dot(
                matrix[:, pl.ds(start, group * block)],
                frame[step, pl.ds(first, group)].reshape(group * block, panel),
                preferred_element_type=jnp.float32,
            )

        if nodes == group:
            add(0)
        else:

            def add_group(index, carry):
                add(index * group)
                return carry

            lax.fori_loop(0, nodes // group, add_group, 0)
        hop_value = acc[...] * scale[...]
        rows[:, pl.ds((step + 1) * panel, panel)] = hop_value.astype(jnp.bfloat16)
        if step + 1 < HOPS:
            put_source(hop_value * scale[...])
    for copy in copies:
        copy.wait_send()


def hops(features, scale, matrix, send_block, block):
    nodes = lax.axis_size("node")
    own_nodes, panel = features.shape
    smem = pl.BlockSpec(memory_space=pltpu.SMEM)
    vmem = pl.BlockSpec(memory_space=pltpu.VMEM)
    dma = pltpu.SemaphoreType.DMA
    return pl.pallas_call(
        functools.partial(hops_kernel, nodes),
        out_shape=jax.ShapeDtypeStruct((own_nodes, (HOPS + 1) * panel), jnp.bfloat16),
        in_specs=[smem, vmem, vmem, vmem],
        out_specs=vmem,
        scratch_shapes=[
            pltpu.VMEM((own_nodes // block, block, panel), jnp.bfloat16),
            pltpu.VMEM((HOPS, nodes - 1, block, panel), jnp.bfloat16),
            pltpu.VMEM((HOPS, nodes, block, panel), jnp.bfloat16),
            pltpu.VMEM((own_nodes, panel), jnp.float32),
            dma((HOPS, nodes - 1)),
            dma((HOPS, nodes - 1)),
        ],
        compiler_params=pltpu.CompilerParams(
            collective_id=1, has_side_effects=True, vmem_limit_bytes=48 * 1024 * 1024
        ),
        cost_estimate=pl.CostEstimate(
            flops=HOPS * 2 * matrix.shape[0] * matrix.shape[1] * panel,
            bytes_accessed=100 * 1024 * 1024,
            transcendentals=0,
        ),
        name="hops",
    )(send_block, features, scale, matrix)


def layer_kernel(
    nodes,
    feats,
    rows_ref,
    weight_ref,
    bias_ref,
    cot_ref,
    out_ref,
    wgrad_ref,
    bgrad_ref,
    pair_send,
    pair_recv,
    held,
    far_send,
    far_recv,
    grad_all,
    block,
    x_send,
    x_recv,
    x_held,
    z_send,
    z_recv,
    bias_all,
    pair_s,
    pair_r,
    far_s,
    far_r,
    gpair_s,
    gpair_r,
    gfar_s,
    gfar_r,
    gfwd_s,
    gfwd_r,
    x_s,
    x_r,
    z_s,
    z_r,
    b_s,
    b_r,
):
    node = lax.axis_index("node")
    feat = lax.axis_index("feat")
    side, high = lax.rem(feat, 2), feat // 2
    highs = feats // 2
    lane, depth = lax.rem(node, 2), node // 2
    depths = nodes // 2
    own_rows = cot_ref.shape[0]
    piece = own_rows // PIECES
    units = wgrad_ref.shape[0]
    pair_feat = feat + 1 - 2 * side

    def far_high(step):
        return lax.rem(high + 1 + step, highs)

    def far_depth(step):
        return lax.rem(depth + 1 + step, depths)

    barrier = pltpu.get_barrier_semaphore()
    pl.semaphore_signal(barrier, inc=1, device_id=(node, pair_feat), device_id_type=MESH)
    for step in range(highs - 1):
        pl.semaphore_signal(
            barrier, inc=1, device_id=(node, far_high(step) * 2 + side), device_id_type=MESH
        )
    for step in range(1, nodes):
        pl.semaphore_signal(
            barrier, inc=1, device_id=(lax.rem(node + step, nodes), feat), device_id_type=MESH
        )
    pl.semaphore_wait(barrier, highs + nodes - 1)

    def terms(owner, part):
        start = pl.multiple_of(owner * own_rows + part * piece, 16)
        return lax.dot_general(
            rows_ref[pl.ds(start, piece), :],
            weight_ref[...],
            (((1,), (1,)), ((), ())),
            preferred_element_type=jnp.float32,
        )

    def remote(src, dst, s, r, device):
        return pltpu.make_async_remote_copy(
            src_ref=src,
            dst_ref=dst,
            send_sem=s,
            recv_sem=r,
            device_id=device,
            device_id_type=MESH,
        )

    pair = (node, pair_feat)
    sends = []
    far_copies = {}
    for step in range(highs):
        for part in range(PIECES):
            slot = step * PIECES + part
            owner = far_high(step) * 2
            pair_send[slot] = terms(owner + 1 - side, part)
            copy = remote(
                pair_send.at[slot], pair_recv.at[slot], pair_s.at[slot], pair_r.at[slot], pair
            )
            copy.start()
            own = terms(owner + side, part)
            copy.wait()
            total = own + pair_recv[slot]
            if step < highs - 1:
                far_send[slot] = total.astype(jnp.bfloat16)
                far = remote(
                    far_send.at[slot],
                    far_recv.at[slot],
                    far_s.at[slot],
                    far_r.at[slot],
                    (node, owner + side),
                )
                far.start()
                far_copies[slot] = far
            else:
                held[part] = total

    def grad_rows(owner, part):
        return pl.ds(pl.multiple_of(owner * own_rows + part * piece, 16), piece)

    for part in range(PIECES):
        linear = held[part]
        for step in range(highs - 1):
            slot = step * PIECES + part
            far_copies[slot].wait()
            linear = linear + far_recv[slot].astype(jnp.float32)
        linear = linear + bias_ref[...]
        gate = 1.0 / (1.0 + jnp.exp(-linear))
        window = pl.ds(part * piece, piece)
        out_ref[window, :] = (linear * gate).astype(jnp.bfloat16)
        grad = cot_ref[window, :].astype(jnp.float32) * gate * (1.0 + linear * (1.0 - gate))
        mine = grad_rows(feat, part)
        grad_all[mine, :] = grad.astype(jnp.bfloat16)
        for step in range(highs - 1):
            slot = step * PIECES + part
            far = remote(
                grad_all.at[mine, :],
                grad_all.at[mine, :],
                gfar_s.at[slot],
                gfar_r.at[slot],
                (node, far_high(step) * 2 + side),
            )
            far.start()
            sends.append(far)
        near = remote(
            grad_all.at[mine, :], grad_all.at[mine, :], gpair_s.at[part], gpair_r.at[part], pair
        )
        near.start()
        sends.append(near)

    forwards = []
    for part in range(PIECES):
        for step in range(highs - 1):
            slot = step * PIECES + part
            origin = lax.rem(high + highs - 1 - step, highs) * 2 + side
            theirs = grad_rows(origin, part)
            remote(
                grad_all.at[theirs, :],
                grad_all.at[theirs, :],
                gfar_s.at[slot],
                gfar_r.at[slot],
                pair,
            ).wait_recv()
            forward = remote(
                grad_all.at[theirs, :],
                grad_all.at[theirs, :],
                gfwd_s.at[slot],
                gfwd_r.at[slot],
                pair,
            )
            forward.start()
            forwards.append(forward)
    for part in range(PIECES):
        other = grad_rows(pair_feat, part)
        remote(
            grad_all.at[other, :], grad_all.at[other, :], gpair_s.at[part], gpair_r.at[part], pair
        ).wait_recv()
        for step in range(highs - 1):
            slot = step * PIECES + part
            origin = lax.rem(high + highs - 1 - step, highs) * 2 + 1 - side
            theirs = grad_rows(origin, part)
            remote(
                grad_all.at[theirs, :],
                grad_all.at[theirs, :],
                gfwd_s.at[slot],
                gfwd_r.at[slot],
                pair,
            ).wait_recv()

    x_pair = (node + 1 - 2 * lane, feat)
    x_copies = []
    z_copies = []

    def finish(step):
        x_copies[step].wait()
        total = x_held[step] + x_recv[step].astype(jnp.float32)
        if step < depths - 1:
            z_send[step] = total.astype(jnp.bfloat16)
            copy = remote(
                z_send.at[step],
                z_recv.at[step],
                z_s.at[step],
                z_r.at[step],
                (far_depth(step) * 2 + lane, feat),
            )
            copy.start()
            z_copies.append(copy)
        else:
            wgrad_ref[...] = total

    def weight_terms(start, count):
        return lax.dot_general(
            grad_all[:, pl.ds(start, count)],
            rows_ref[...],
            (((0,), (0,)), ((), ())),
            preferred_element_type=jnp.float32,
        )

    outs = grad_all.shape[1]
    aligned = (2 * units) % 128 == 0
    if not aligned:
        for start in range(0, outs, 128):
            block[pl.ds(start, 128), :] = weight_terms(start, 128)

    b_copies = []
    for step in range(depths):
        start = pl.multiple_of(far_depth(step) * (2 * units), 2 * units)
        if aligned:
            block[...] = weight_terms(start, 2 * units)
            start = 0
        theirs = pl.ds(pl.multiple_of(start + (1 - lane) * units, 16), units)
        mine = pl.ds(pl.multiple_of(start + lane * units, 16), units)
        x_send[step] = block[theirs, :].astype(jnp.bfloat16)
        copy = remote(x_send.at[step], x_recv.at[step], x_s.at[step], x_r.at[step], x_pair)
        copy.start()
        x_copies.append(copy)
        x_held[step] = block[mine, :]
        if step == 0:
            bias_all[node] = jnp.sum(grad_all[...].astype(jnp.float32), axis=0, keepdims=True)
            for hop in range(1, nodes):
                copy = remote(
                    bias_all.at[node],
                    bias_all.at[node],
                    b_s.at[hop - 1],
                    b_r.at[hop - 1],
                    (lax.rem(node + hop, nodes), feat),
                )
                copy.start()
                b_copies.append(copy)
        else:
            finish(step - 1)
    finish(depths - 1)

    for hop in range(1, nodes):
        sender = lax.rem(node + nodes - hop, nodes)
        remote(
            bias_all.at[sender],
            bias_all.at[sender],
            b_s.at[hop - 1],
            b_r.at[hop - 1],
            (lax.rem(node + hop, nodes), feat),
        ).wait_recv()
    bias_total = bias_all[0]
    for part in range(1, nodes):
        bias_total = bias_total + bias_all[part]
    bgrad_ref[...] = bias_total

    for step in range(depths - 1):
        z_copies[step].wait()
        wgrad_ref[...] += z_recv[step].astype(jnp.float32)
    for copy in sends + forwards + b_copies:
        copy.wait_send()


def layer(rows, flat_weight, out_bias, cotangent):
    nodes, feats = lax.axis_size("node"), lax.axis_size("feat")
    highs, depths = feats // 2, nodes // 2
    total_rows, width = rows.shape
    outs = flat_weight.shape[0]
    own_rows = cotangent.shape[0]
    units = outs // nodes
    piece = own_rows // PIECES
    block_rows = 2 * units if (2 * units) % 128 == 0 else outs
    slots = highs * PIECES
    far_slots = max(1, (highs - 1) * PIECES)
    z_slots = max(1, depths - 1)
    dma = pltpu.SemaphoreType.DMA
    vmem = pl.BlockSpec(memory_space=pltpu.VMEM)
    flops = 4 * total_rows * width * outs
    return pl.pallas_call(
        functools.partial(layer_kernel, nodes, feats),
        out_shape=(
            jax.ShapeDtypeStruct((own_rows, outs), jnp.bfloat16),
            jax.ShapeDtypeStruct((units, width), jnp.float32),
            jax.ShapeDtypeStruct((1, outs), jnp.float32),
        ),
        in_specs=[vmem] * 4,
        out_specs=(vmem,) * 3,
        scratch_shapes=[
            pltpu.VMEM((slots, piece, outs), jnp.float32),
            pltpu.VMEM((slots, piece, outs), jnp.float32),
            pltpu.VMEM((PIECES, piece, outs), jnp.float32),
            pltpu.VMEM((far_slots, piece, outs), jnp.bfloat16),
            pltpu.VMEM((far_slots, piece, outs), jnp.bfloat16),
            pltpu.VMEM((total_rows, outs), jnp.bfloat16),
            pltpu.VMEM((block_rows, width), jnp.float32),
            pltpu.VMEM((depths, units, width), jnp.bfloat16),
            pltpu.VMEM((depths, units, width), jnp.bfloat16),
            pltpu.VMEM((depths, units, width), jnp.float32),
            pltpu.VMEM((z_slots, units, width), jnp.bfloat16),
            pltpu.VMEM((z_slots, units, width), jnp.bfloat16),
            pltpu.VMEM((nodes, 1, outs), jnp.float32),
            dma((slots,)),
            dma((slots,)),
            dma((far_slots,)),
            dma((far_slots,)),
            dma((PIECES,)),
            dma((PIECES,)),
            dma((far_slots,)),
            dma((far_slots,)),
            dma((far_slots,)),
            dma((far_slots,)),
            dma((depths,)),
            dma((depths,)),
            dma((z_slots,)),
            dma((z_slots,)),
            dma((nodes,)),
            dma((nodes,)),
        ],
        compiler_params=pltpu.CompilerParams(
            collective_id=0, has_side_effects=True, vmem_limit_bytes=48 * 1024 * 1024
        ),
        cost_estimate=pl.CostEstimate(
            flops=flops, bytes_accessed=8 * total_rows * outs, transcendentals=own_rows * outs
        ),
        name="layer",
    )(rows, flat_weight, out_bias[None, :], cotangent)


def local(
    features,
    degrees,
    tile_row,
    tile_col,
    tile_count,
    send_block,
    tile_val,
    weight,
    out_bias,
    cotangent,
):
    row_scale = lax.rsqrt(degrees.astype(jnp.float32))[:, None]
    flat_weight = lax.all_gather(weight.reshape(weight.shape[0], -1), "node", axis=0, tiled=True)
    matrix = dense_matrix(tile_row, tile_col, tile_count, tile_val, features.shape[0])
    rows = hops(features, row_scale, matrix, send_block, tile_val.shape[-1])
    output, weight_grad, bias_grad = layer(rows, flat_weight, out_bias, cotangent)
    return (output, weight_grad.reshape(weight.shape), bias_grad[0])


def solution(mesh):
    in_specs = (
        P("node", "feat"),
        P("node"),
        P("node", None),
        P("node", None),
        P("node"),
        P(),
        P("node", None, None, None),
        P("node", None, "feat"),
        P(),
        P(("node", "feat"), None),
    )
    out_specs = (P(("node", "feat"), None), P("node", None, "feat"), P())
    return jax.shard_map(local, mesh=mesh, in_specs=in_specs, out_specs=out_specs, check_vma=False)
```

time: 249 us -> 128 us (0.51)
  waiting for transfers between devices: 124 us -> 15.2 us
  Pallas kernels: 0 us -> 89.3 us
  blocking collectives: 41.2 us -> 0 us
  matrix products: 26.4 us -> 0 us
  local copies, waits for them, and re-layouts: 22.8 us -> 7.41 us
  starting transfers between devices: 11.7 us -> 0.04 us
  other arithmetic: 7.83 us -> 0.69 us
    pallas_call x0 -> x3, Pallas kernels: none -> 89.3 us  [the longest x1 52.6 us: layer(): pl.pallas_call(functools.partial(layer_kernel, nodes, feats), out_shape=(...]
    reduce_scatter x2 -> x0, waiting for transfers between devices: 71.8 us -> none  [the longest x1 36.7 us: local(): lax.psum_scatter(panel_terms, 'feat', scatter_dimension=0, tiled=True)]
    psum x1 -> x0, blocking collectives: 41.2 us -> none  [local(): lax.psum(jnp.sum(grad_linear.astype(jnp.float32), axis=0), ('node', 'feat'))]
    all_to_all x2 -> x0, waiting for transfers between devices: 32.7 us -> none  [propagate(): lax.all_to_all(outgoing, 'node', split_axis=0, concat_axis=0, tiled=True)]
    dot_general x6 -> x0, matrix products: 26.4 us -> none  [the longest x2 8.88 us: propagate(): jnp.einsum('tij,tjc->tic', tile_values, sources, preferred_element_type=j...]
    dot_general x4 -> x0, local copies, waits for them, and re-layouts: 13 us -> none  [the longest x2 11.6 us: propagate(): jnp.einsum('tij,tjc->tic', tile_values, sources, preferred_element_type=j...]
    all_to_all x2 -> x0, starting transfers between devices: 11.4 us -> none  [propagate(): lax.all_to_all(outgoing, 'node', split_axis=0, concat_axis=0, tiled=True)]
    gather x4 -> x0, local copies, waits for them, and re-layouts: 7.24 us -> none  [the longest x2 4.49 us: propagate(): sources = frame[tile_cols]]
  transfers between devices with their start and end apart: 6 -> 1, of which waited for: 5 -> 1; matrix products, arithmetic and copies ran while one was open for 16% -> 1% of each run, Pallas kernels for 0% -> 29%
where the time goes in v1:
time: 128 us; the launch traced here: 127 us
  Pallas kernels  89.3 us (70%)
  waiting for transfers between devices  15.2 us (12%)
  between operations  14.7 us (11%)
  local copies, waits for them, and re-layouts  7.41 us (6%)
    pallas_call x1, Pallas kernels, layer(): pl.pallas_call(functools.partial(layer_kernel, nodes, feats), out_shape=(...  52.6 us
    pallas_call x1, Pallas kernels, hops(): pl.pallas_call(functools.partial(hops_kernel, nodes), out_shape=jax.Shape...  35.6 us
    all_gather x1, waiting for transfers between devices, local(): lax.all_gather(weight.reshape(weight.shape[0], -1), 'node', axis=0, tiled...  15.2 us
    unnamed x20, local copies, waits for them, and re-layouts  6.26 us
  transfers between devices with their start and end apart: 1, of which 1 were waited for; matrix products, arithmetic and copies ran while one was open for 1% of the time, Pallas kernels for 29%

profile of v1, /device:TPU:0, one launch (start us, length us, event | category | flops | bytes accessed | tf_op | source)
XLA Modules:
  0.0 127.4 jit_solution(2725417782955453146)
XLA Ops:
  7.2 0.0 copy-start
  7.2 0.0 all-gather.2.cloned.1.call-start
  7.2 1.2 copy.16
  8.4 0.8 copy.17
  9.2 0.0 all-gather.2.cloned.1.call-update
  9.9 0.7 convert_rsqrt_fusion
  10.6 0.2 broadcast_in_dim.8.scale
  10.8 0.0 copy-done
  10.8 0.0 copy-start.1
  10.8 0.6 copy-done.1
  11.4 0.7 copy-done.2
  12.1 1.0 matrix.1
  13.1 0.1 copy-done.4
  13.2 0.0 copy-done.6
  13.2 35.6 %hops.1.rows_ref = bf16[768,768]{1,0:T(8,128)(2,1)S(1)} custom-call(s32[8,8]{1,0:T(8,128)S(1)} %copy-done.6, f32[768,256]{1,0:T(8,128)S(1)} %copy-done.4, f32[768,1]{1,0:T(8,128)S(1)} %broadcast_in_dim.8.scale, bf16[768,1792]{1,0:T(8,128)(2,1)S(1)} %matrix.1), custom_call_target="tpu_custom_call" | custom-call | flops 1409286144 | bytes 104857600 | tf_op jit(solution)/shard_map/hops/pallas_call | solution.py:133
  48.9 15.2 %all-gather.2.cloned.1.call-done.weight_ref = bf16[1024,768]{1,0:T(8,128)(2,1)} async-done(((bf16[128,768]{1,0:T(8,128)(2,1)}), bf16[1024,768]{1,0:T(8,128)(2,1)}) %all-gather.2.cloned.1.call-update) | async-done | bytes 1572880 | tf_op jit(solution)/shard_map/all_gather | solution.py:510
  64.1 0.0 copy-done.5
  64.1 0.0 copy-done.7
  64.1 1.4 %copy-done.3 = bf16[1024,768]{1,0:T(8,128)(2,1)S(1)} copy-done((bf16[1024,768]{1,0:T(8,128)(2,1)S(1)}, bf16[1024,768]{1,0:T(8,128)(2,1)}, u32[]{:S(2)}) %copy-start.3) | copy-done | bytes 1572888
  65.5 52.6 %layer.1 = (bf16[192,1024]{1,0:T(8,128)(2,1)S(1)}, f32[128,768]{1,0:T(8,128)S(1)}, f32[1,1024]{1,0:T(1,128)S(1)}) custom-call(bf16[768,768]{1,0:T(8,128)(2,1)S(1)} %hops.1.rows_ref, bf16[1024,768]{1,0:T(8,128)(2,1)S(1)} %copy-done.3, f32[1,1024]{1,0:T(1,128)S(1)} %bitcast.5, bf16[192,1024]{1,0:T(8,128)(2,1)S(1)} %copy-done.5), custom_call_target="tpu_custom_call" | custom-call | flops 2415919104 | bytes 6291456 | tf_op jit(solution)/shard_map/layer/pallas_call | solution.py:447
  118.1 0.2 copy.18
  118.3 0.9 copy.19
  119.2 0.7 copy.23
  119.9 0.6 copy.24
  (6 shorter events, 0.0 us)
Async XLA Ops:
  7.2 3.6 %copy-start = (bf16[1,33,128,128]{3,2,1,0:T(8,128)(2,1)S(1)}, bf16[1,33,128,128]{3,2,1,0:T(8,128)(2,1)}, u32[]{:S(2)}) copy-start(bf16[1,33,128,128]{3,2,1,0:T(8,128)(2,1)} %tile_val.1) | copy-start | bytes 3244036
  7.2 56.9 %all-gather.2.cloned.1.call-start = ((), (), s32[]{:S(2)}) async-start(), calls=%async_computation | async-start | bytes 1769472 | tf_op jit(solution)/shard_map/all_gather | solution.py:510
  10.8 0.7 copy-start.1
  11.4 0.7 copy-start.2
  12.1 1.1 copy-start.4
  12.1 1.1 copy-start.6
  13.2 50.9 %copy-start.5 = (bf16[192,1024]{1,0:T(8,128)(2,1)S(1)}, bf16[192,1024]{1,0:T(8,128)(2,1)}, u32[]{:S(2)}) copy-start(bf16[192,1024]{1,0:T(8,128)(2,1)} %cot_ref.1) | copy-start | bytes 1179652
  13.2 50.9 %copy-start.7 = (f32[1024]{0:T(1024)S(1)}, f32[1024]{0:T(1024)}, u32[]{:S(2)}) copy-start(f32[1024]{0:T(1024)} %param.18) | copy-start | bytes 12292
  64.1 1.4 %copy-start.3 = (bf16[1024,768]{1,0:T(8,128)(2,1)S(1)}, bf16[1024,768]{1,0:T(8,128)(2,1)}, u32[]{:S(2)}) copy-start(bf16[1024,768]{1,0:T(8,128)(2,1)} %all-gather.2.cloned.1.call-done.weight_ref) | copy-start | bytes 4718596
Sparse Core Ops, SparseCore 0:
  10.8 53.2 all-gather.1

commit v2 on v1

--- a/solution.py
+++ b/solution.py
@@ -8,7 +8,6 @@
 from jax.sharding import PartitionSpec as P
 
 HOPS = 2
-PIECES = 2
 MESH = pl.DeviceIdType.MESH
 
 
@@ -158,6 +157,7 @@
 def layer_kernel(
     nodes,
     feats,
+    cols,
     rows_ref,
     weight_ref,
     bias_ref,
@@ -165,7 +165,7 @@
     out_ref,
     wgrad_ref,
     bgrad_ref,
-    pair_send,
+    terms,
     pair_recv,
     held,
     far_send,
@@ -200,38 +200,26 @@
     side, high = lax.rem(feat, 2), feat // 2
     highs = feats // 2
     lane, depth = lax.rem(node, 2), node // 2
-    depths = nodes // 2
     own_rows = cot_ref.shape[0]
-    piece = own_rows // PIECES
     units = wgrad_ref.shape[0]
-    pair_feat = feat + 1 - 2 * side
-
-    def far_high(step):
-        return lax.rem(high + 1 + step, highs)
-
-    def far_depth(step):
-        return lax.rem(depth + 1 + step, depths)
-
-    barrier = pltpu.get_barrier_semaphore()
-    pl.semaphore_signal(barrier, inc=1, device_id=(node, pair_feat), device_id_type=MESH)
-    for step in range(highs - 1):
-        pl.semaphore_signal(
-            barrier, inc=1, device_id=(node, far_high(step) * 2 + side), device_id_type=MESH
-        )
-    for step in range(1, nodes):
-        pl.semaphore_signal(
-            barrier, inc=1, device_id=(lax.rem(node + step, nodes), feat), device_id_type=MESH
-        )
-    pl.semaphore_wait(barrier, highs + nodes - 1)
-
-    def terms(owner, part):
-        start = pl.multiple_of(owner * own_rows + part * piece, 16)
-        return lax.dot_general(
-            rows_ref[pl.ds(start, piece), :],
-            weight_ref[...],
-            (((1,), (1,)), ((), ())),
-            preferred_element_type=jnp.float32,
-        )
+    pieces = weight_ref.shape[0] // cols
+    share = cols // (2 * units)
+    pair = (node, feat + 1 - 2 * side)
+    x_pair = (node + 1 - 2 * lane, feat)
+
+    def far_feat(step):
+        return lax.rem(high + 1 + step, highs) * 2 + side
+
+    def window(index):
+        piece = lax.rem(depth // share + 1 + index, pieces)
+        return pl.ds(pl.multiple_of(piece * cols, cols), cols)
+
+    def target(index, sub):
+        piece = lax.rem(depth // share + 1 + index, pieces)
+        return piece * share + lax.rem(lax.rem(depth, share) + 1 + sub, share)
+
+    def chunk(owner):
+        return pl.ds(pl.multiple_of(owner * own_rows, 16), own_rows)
 
     def remote(src, dst, s, r, device):
         return pltpu.make_async_remote_copy(
@@ -243,157 +231,125 @@
             device_id_type=MESH,
         )
 
-    pair = (node, pair_feat)
-    sends = []
+    barrier = pltpu.get_barrier_semaphore()
+    pl.semaphore_signal(barrier, inc=1, device_id=pair, device_id_type=MESH)
+    for step in range(highs - 1):
+        pl.semaphore_signal(
+            barrier, inc=1, device_id=(node, far_feat(step)), device_id_type=MESH
+        )
+    for step in range(1, nodes):
+        pl.semaphore_signal(
+            barrier, inc=1, device_id=(lax.rem(node + step, nodes), feat), device_id_type=MESH
+        )
+
+    started = []
+    pair_copies = {}
     far_copies = {}
-    for step in range(highs):
-        for part in range(PIECES):
-            slot = step * PIECES + part
-            owner = far_high(step) * 2
-            pair_send[slot] = terms(owner + 1 - side, part)
+    near_grads = {}
+    far_grads = {}
+    x_copies = {}
+    z_copies = []
+
+    def make_terms(index):
+        terms[index] = lax.dot_general(
+            rows_ref[...],
+            weight_ref[window(index), :],
+            (((1,), (1,)), ((), ())),
+            preferred_element_type=jnp.float32,
+        )
+        if index == 0:
+            pl.semaphore_wait(barrier, highs + nodes - 1)
+        for top in range(highs):
             copy = remote(
-                pair_send.at[slot], pair_recv.at[slot], pair_s.at[slot], pair_r.at[slot], pair
-            )
-            copy.start()
-            own = terms(owner + side, part)
-            copy.wait()
-            total = own + pair_recv[slot]
-            if step < highs - 1:
-                far_send[slot] = total.astype(jnp.bfloat16)
-                far = remote(
-                    far_send.at[slot],
-                    far_recv.at[slot],
-                    far_s.at[slot],
-                    far_r.at[slot],
-                    (node, owner + side),
-                )
-                far.start()
-                far_copies[slot] = far
-            else:
-                held[part] = total
-
-    def grad_rows(owner, part):
-        return pl.ds(pl.multiple_of(owner * own_rows + part * piece, 16), piece)
-
-    for part in range(PIECES):
-        linear = held[part]
+                terms.at[index, chunk(top * 2 + 1 - side), :],
+                pair_recv.at[index, top],
+                pair_s.at[index, top],
+                pair_r.at[index, top],
+                pair,
+            )
+            copy.start()
+            pair_copies[index, top] = copy
+
+    def add_pair(index):
+        for top in range(highs):
+            pair_copies[index, top].wait()
         for step in range(highs - 1):
-            slot = step * PIECES + part
-            far_copies[slot].wait()
-            linear = linear + far_recv[slot].astype(jnp.float32)
-        linear = linear + bias_ref[...]
+            owner = far_feat(step)
+            total = terms[index, chunk(owner), :] + pair_recv[index, owner // 2]
+            far_send[index, step] = total.astype(jnp.bfloat16)
+            copy = remote(
+                far_send.at[index, step],
+                far_recv.at[index, step],
+                far_s.at[index, step],
+                far_r.at[index, step],
+                (node, owner),
+            )
+            copy.start()
+            far_copies[index, step] = copy
+        held[index] = terms[index, chunk(feat), :] + pair_recv[index, high]
+
+    def make_grad(index):
+        linear = held[index]
+        for step in range(highs - 1):
+            far_copies[index, step].wait()
+            linear = linear + far_recv[index, step].astype(jnp.float32)
+        linear = linear + bias_ref[:, window(index)]
         gate = 1.0 / (1.0 + jnp.exp(-linear))
-        window = pl.ds(part * piece, piece)
-        out_ref[window, :] = (linear * gate).astype(jnp.bfloat16)
-        grad = cot_ref[window, :].astype(jnp.float32) * gate * (1.0 + linear * (1.0 - gate))
-        mine = grad_rows(feat, part)
-        grad_all[mine, :] = grad.astype(jnp.bfloat16)
+        out_ref[:, window(index)] = (linear * gate).astype(jnp.bfloat16)
+        slope = gate * (1.0 + linear * (1.0 - gate))
+        grad = cot_ref[:, window(index)].astype(jnp.float32) * slope
+        grad_all[index, chunk(feat), :] = grad.astype(jnp.bfloat16)
+        mine = grad_all.at[index, chunk(feat), :]
         for step in range(highs - 1):
-            slot = step * PIECES + part
-            far = remote(
-                grad_all.at[mine, :],
-                grad_all.at[mine, :],
-                gfar_s.at[slot],
-                gfar_r.at[slot],
-                (node, far_high(step) * 2 + side),
-            )
-            far.start()
-            sends.append(far)
-        near = remote(
-            grad_all.at[mine, :], grad_all.at[mine, :], gpair_s.at[part], gpair_r.at[part], pair
-        )
-        near.start()
-        sends.append(near)
-
-    forwards = []
-    for part in range(PIECES):
+            copy = remote(
+                mine, mine, gfar_s.at[index, step], gfar_r.at[index, step], (node, far_feat(step))
+            )
+            copy.start()
+            started.append(copy)
+        copy = remote(mine, mine, gpair_s.at[index], gpair_r.at[index], pair)
+        copy.start()
+        started.append(copy)
+
+    def forward_grad(index):
         for step in range(highs - 1):
-            slot = step * PIECES + part
             origin = lax.rem(high + highs - 1 - step, highs) * 2 + side
-            theirs = grad_rows(origin, part)
+            theirs = grad_all.at[index, chunk(origin), :]
             remote(
-                grad_all.at[theirs, :],
-                grad_all.at[theirs, :],
-                gfar_s.at[slot],
-                gfar_r.at[slot],
-                pair,
+                theirs, theirs, gfar_s.at[index, step], gfar_r.at[index, step], pair
             ).wait_recv()
-            forward = remote(
-                grad_all.at[theirs, :],
-                grad_all.at[theirs, :],
-                gfwd_s.at[slot],
-                gfwd_r.at[slot],
-                pair,
-            )
-            forward.start()
-            forwards.append(forward)
-    for part in range(PIECES):
-        other = grad_rows(pair_feat, part)
-        remote(
-            grad_all.at[other, :], grad_all.at[other, :], gpair_s.at[part], gpair_r.at[part], pair
-        ).wait_recv()
+            copy = remote(theirs, theirs, gfwd_s.at[index, step], gfwd_r.at[index, step], pair)
+            copy.start()
+            started.append(copy)
+
+    def weight_terms(index):
+        other = grad_all.at[index, chunk(feat + 1 - 2 * side), :]
+        remote(other, other, gpair_s.at[index], gpair_r.at[index], pair).wait_recv()
         for step in range(highs - 1):
-            slot = step * PIECES + part
             origin = lax.rem(high + highs - 1 - step, highs) * 2 + 1 - side
-            theirs = grad_rows(origin, part)
+            theirs = grad_all.at[index, chunk(origin), :]
             remote(
-                grad_all.at[theirs, :],
-                grad_all.at[theirs, :],
-                gfwd_s.at[slot],
-                gfwd_r.at[slot],
-                pair,
+                theirs, theirs, gfwd_s.at[index, step], gfwd_r.at[index, step], pair
             ).wait_recv()
-
-    x_pair = (node + 1 - 2 * lane, feat)
-    x_copies = []
-    z_copies = []
-
-    def finish(step):
-        x_copies[step].wait()
-        total = x_held[step] + x_recv[step].astype(jnp.float32)
-        if step < depths - 1:
-            z_send[step] = total.astype(jnp.bfloat16)
-            copy = remote(
-                z_send.at[step],
-                z_recv.at[step],
-                z_s.at[step],
-                z_r.at[step],
-                (far_depth(step) * 2 + lane, feat),
-            )
-            copy.start()
-            z_copies.append(copy)
-        else:
-            wgrad_ref[...] = total
-
-    def weight_terms(start, count):
-        return lax.dot_general(
-            grad_all[:, pl.ds(start, count)],
+        block[...] = lax.dot_general(
+            grad_all[index],
             rows_ref[...],
             (((0,), (0,)), ((), ())),
             preferred_element_type=jnp.float32,
         )
-
-    outs = grad_all.shape[1]
-    aligned = (2 * units) % 128 == 0
-    if not aligned:
-        for start in range(0, outs, 128):
-            block[pl.ds(start, 128), :] = weight_terms(start, 128)
-
-    b_copies = []
-    for step in range(depths):
-        start = pl.multiple_of(far_depth(step) * (2 * units), 2 * units)
-        if aligned:
-            block[...] = weight_terms(start, 2 * units)
-            start = 0
-        theirs = pl.ds(pl.multiple_of(start + (1 - lane) * units, 16), units)
-        mine = pl.ds(pl.multiple_of(start + lane * units, 16), units)
-        x_send[step] = block[theirs, :].astype(jnp.bfloat16)
-        copy = remote(x_send.at[step], x_recv.at[step], x_s.at[step], x_r.at[step], x_pair)
-        copy.start()
-        x_copies.append(copy)
-        x_held[step] = block[mine, :]
-        if step == 0:
-            bias_all[node] = jnp.sum(grad_all[...].astype(jnp.float32), axis=0, keepdims=True)
+        for sub in range(share):
+            slot = index * share + sub
+            start = lax.rem(lax.rem(depth, share) + 1 + sub, share) * (2 * units)
+            theirs = pl.ds(pl.multiple_of(start + (1 - lane) * units, 16), units)
+            mine = pl.ds(pl.multiple_of(start + lane * units, 16), units)
+            x_send[slot] = block[theirs, :].astype(jnp.bfloat16)
+            copy = remote(x_send.at[slot], x_recv.at[slot], x_s.at[slot], x_r.at[slot], x_pair)
+            copy.start()
+            x_copies[slot] = copy
+            x_held[slot] = block[mine, :]
+        bias_all[node, :, window(index)] = jnp.sum(
+            grad_all[index].astype(jnp.float32), axis=0, keepdims=True
+        )
+        if index == pieces - 1:
             for hop in range(1, nodes):
                 copy = remote(
                     bias_all.at[node],
@@ -403,10 +359,32 @@
                     (lax.rem(node + hop, nodes), feat),
                 )
                 copy.start()
-                b_copies.append(copy)
-        else:
-            finish(step - 1)
-    finish(depths - 1)
+                started.append(copy)
+
+    def add_x(index):
+        for sub in range(share):
+            slot = index * share + sub
+            x_copies[slot].wait()
+            total = x_held[slot] + x_recv[slot].astype(jnp.float32)
+            if slot == pieces * share - 1:
+                wgrad_ref[...] = total
+                continue
+            z_send[slot] = total.astype(jnp.bfloat16)
+            copy = remote(
+                z_send.at[slot],
+                z_recv.at[slot],
+                z_s.at[slot],
+                z_r.at[slot],
+                (target(index, sub) * 2 + lane, feat),
+            )
+            copy.start()
+            z_copies.append(copy)
+
+    stages = (make_terms, add_pair, make_grad, forward_grad, weight_terms, add_x)
+    for tick in range(pieces + len(stages) - 1):
+        for order, stage in enumerate(stages):
+            if 0 <= tick - order < pieces:
+                stage(tick - order)
 
     for hop in range(1, nodes):
         sender = lax.rem(node + nodes - hop, nodes)
@@ -422,10 +400,10 @@
         bias_total = bias_total + bias_all[part]
     bgrad_ref[...] = bias_total
 
-    for step in range(depths - 1):
-        z_copies[step].wait()
-        wgrad_ref[...] += z_recv[step].astype(jnp.float32)
-    for copy in sends + forwards + b_copies:
+    for slot, copy in enumerate(z_copies):
+        copy.wait()
+        wgrad_ref[...] += z_recv[slot].astype(jnp.float32)
+    for copy in started:
         copy.wait_send()
 
 
@@ -436,16 +414,14 @@
     outs = flat_weight.shape[0]
     own_rows = cotangent.shape[0]
     units = outs // nodes
-    piece = own_rows // PIECES
-    block_rows = 2 * units if (2 * units) % 128 == 0 else outs
-    slots = highs * PIECES
-    far_slots = max(1, (highs - 1) * PIECES)
-    z_slots = max(1, depths - 1)
+    cols = max(2 * units, 128)
+    pieces = outs // cols
+    fars = max(1, highs - 1)
     dma = pltpu.SemaphoreType.DMA
     vmem = pl.BlockSpec(memory_space=pltpu.VMEM)
     flops = 4 * total_rows * width * outs
     return pl.pallas_call(
-        functools.partial(layer_kernel, nodes, feats),
+        functools.partial(layer_kernel, nodes, feats, cols),
         out_shape=(
             jax.ShapeDtypeStruct((own_rows, outs), jnp.bfloat16),
             jax.ShapeDtypeStruct((units, width), jnp.float32),
@@ -454,33 +430,33 @@
         in_specs=[vmem] * 4,
         out_specs=(vmem,) * 3,
         scratch_shapes=[
-            pltpu.VMEM((slots, piece, outs), jnp.float32),
-            pltpu.VMEM((slots, piece, outs), jnp.float32),
-            pltpu.VMEM((PIECES, piece, outs), jnp.float32),
-            pltpu.VMEM((far_slots, piece, outs), jnp.bfloat16),
-            pltpu.VMEM((far_slots, piece, outs), jnp.bfloat16),
-            pltpu.VMEM((total_rows, outs), jnp.bfloat16),
-            pltpu.VMEM((block_rows, width), jnp.float32),
+            pltpu.VMEM((pieces, total_rows, cols), jnp.float32),
+            pltpu.VMEM((pieces, highs, own_rows, cols), jnp.float32),
+            pltpu.VMEM((pieces, own_rows, cols), jnp.float32),
+            pltpu.VMEM((pieces, fars, own_rows, cols), jnp.bfloat16),
+            pltpu.VMEM((pieces, fars, own_rows, cols), jnp.bfloat16),
+            pltpu.VMEM((pieces, total_rows, cols), jnp.bfloat16),
+            pltpu.VMEM((cols, width), jnp.float32),
             pltpu.VMEM((depths, units, width), jnp.bfloat16),
             pltpu.VMEM((depths, units, width), jnp.bfloat16),
             pltpu.VMEM((depths, units, width), jnp.float32),
-            pltpu.VMEM((z_slots, units, width), jnp.bfloat16),
-            pltpu.VMEM((z_slots, units, width), jnp.bfloat16),
+            pltpu.VMEM((depths, units, width), jnp.bfloat16),
+            pltpu.VMEM((depths, units, width), jnp.bfloat16),
             pltpu.VMEM((nodes, 1, outs), jnp.float32),
-            dma((slots,)),
-            dma((slots,)),
-            dma((far_slots,)),
-            dma((far_slots,)),
-            dma((PIECES,)),
-            dma((PIECES,)),
-            dma((far_slots,)),
-            dma((far_slots,)),
-            dma((far_slots,)),
-            dma((far_slots,)),
+            dma((pieces, highs)),
+            dma((pieces, highs)),
+            dma((pieces, fars)),
+            dma((pieces, fars)),
+            dma((pieces,)),
+            dma((pieces,)),
+            dma((pieces, fars)),
+            dma((pieces, fars)),
+            dma((pieces, fars)),
+            dma((pieces, fars)),
             dma((depths,)),
             dma((depths,)),
-            dma((z_slots,)),
-            dma((z_slots,)),
+            dma((depths,)),
+            dma((depths,)),
             dma((nodes,)),
             dma((nodes,)),
         ],

time: 128 us -> 117 us (0.914)
  Pallas kernels: 89.3 us -> 81.9 us
  waiting for transfers between devices: 15.2 us -> 12 us
    pallas_call x1, Pallas kernels: 52.6 us -> 42.1 us  [layer(): pl.pallas_call(functools.partial(layer_kernel, nodes, feats, cols), out_s...]
    all_gather x1, waiting for transfers between devices: 15.2 us -> 12 us  [local(): lax.all_gather(weight.reshape(weight.shape[0], -1), 'node', axis=0, tiled...]
    pallas_call x1, Pallas kernels: 35.6 us -> 38.7 us  [hops(): pl.pallas_call(functools.partial(hops_kernel, nodes), out_shape=jax.Shape...]
  transfers between devices with their start and end apart: 1 -> 1, of which waited for: 1 -> 1; matrix products, arithmetic and copies ran while one was open for 1% -> 1% of each run, Pallas kernels for 29% -> 34%
where the time goes in v2:
time: 117 us
  Pallas kernels  81.9 us (70%)
  between operations  14.7 us (13%)
  waiting for transfers between devices  12 us (10%)
  local copies, waits for them, and re-layouts  7.34 us (6%)
    pallas_call x1, Pallas kernels, layer(): pl.pallas_call(functools.partial(layer_kernel, nodes, feats, cols), out_s...  42.1 us
    pallas_call x1, Pallas kernels, hops(): pl.pallas_call(functools.partial(hops_kernel, nodes), out_shape=jax.Shape...  38.7 us
    all_gather x1, waiting for transfers between devices, local(): lax.all_gather(weight.reshape(weight.shape[0], -1), 'node', axis=0, tiled...  12 us
    unnamed x20, local copies, waits for them, and re-layouts  6.19 us
  transfers between devices with their start and end apart: 1, of which 1 were waited for; matrix products, arithmetic and copies ran while one was open for 1% of the time, Pallas kernels for 34%

profile of v2, /device:TPU:0, one launch (start us, length us, event | category | flops | bytes accessed | tf_op | source)
XLA Modules:
  0.0 116.7 jit_solution(1090492192843386722)
XLA Ops:
  7.2 0.0 copy-start
  7.2 0.0 all-gather.2.cloned.1.call-start
  7.2 1.2 copy.16
  8.4 0.8 copy.17
  9.2 0.0 all-gather.2.cloned.1.call-update
  9.9 0.7 convert_rsqrt_fusion
  10.6 0.2 broadcast_in_dim.8.scale
  10.8 0.0 copy-done
  10.8 0.0 copy-start.1
  10.8 0.6 copy-done.1
  11.4 0.7 copy-done.2
  12.1 1.1 matrix.1
  13.2 0.0 copy-done.4
  13.2 0.0 copy-done.6
  13.2 38.7 %hops.1.rows_ref = bf16[768,768]{1,0:T(8,128)(2,1)S(1)} custom-call(s32[8,8]{1,0:T(8,128)S(1)} %copy-done.6, f32[768,256]{1,0:T(8,128)S(1)} %copy-done.4, f32[768,1]{1,0:T(8,128)S(1)} %broadcast_in_dim.8.scale, bf16[768,1792]{1,0:T(8,128)(2,1)S(1)} %matrix.1), custom_call_target="tpu_custom_call" | custom-call | flops 1409286144 | bytes 104857600 | tf_op jit(solution)/shard_map/hops/pallas_call | solution.py:132
  51.9 12.0 %all-gather.2.cloned.1.call-done.weight_ref = bf16[1024,768]{1,0:T(8,128)(2,1)} async-done(((bf16[128,768]{1,0:T(8,128)(2,1)}), bf16[1024,768]{1,0:T(8,128)(2,1)}) %all-gather.2.cloned.1.call-update) | async-done | bytes 1572880 | tf_op jit(solution)/shard_map/all_gather | solution.py:486
  63.9 0.0 copy-done.5
  63.9 0.0 copy-done.7
  63.9 1.4 %copy-done.3 = bf16[1024,768]{1,0:T(8,128)(2,1)S(1)} copy-done((bf16[1024,768]{1,0:T(8,128)(2,1)S(1)}, bf16[1024,768]{1,0:T(8,128)(2,1)}, u32[]{:S(2)}) %copy-start.3) | copy-done | bytes 1572888
  65.3 42.1 %layer.1 = (bf16[192,1024]{1,0:T(8,128)(2,1)S(1)}, f32[128,768]{1,0:T(8,128)S(1)}, f32[1,1024]{1,0:T(1,128)S(1)}) custom-call(bf16[768,768]{1,0:T(8,128)(2,1)S(1)} %hops.1.rows_ref, bf16[1024,768]{1,0:T(8,128)(2,1)S(1)} %copy-done.3, f32[1,1024]{1,0:T(1,128)S(1)} %bitcast.5, bf16[192,1024]{1,0:T(8,128)(2,1)S(1)} %copy-done.5), custom_call_target="tpu_custom_call" | custom-call | flops 2415919104 | bytes 6291456 | tf_op jit(solution)/shard_map/layer/pallas_call | solution.py:423
  107.4 0.2 copy.18
  107.6 0.9 copy.19
  108.5 0.7 copy.23
  109.3 0.6 copy.24
  (6 shorter events, 0.0 us)
Async XLA Ops:
  7.2 3.6 %copy-start = (bf16[1,33,128,128]{3,2,1,0:T(8,128)(2,1)S(1)}, bf16[1,33,128,128]{3,2,1,0:T(8,128)(2,1)}, u32[]{:S(2)}) copy-start(bf16[1,33,128,128]{3,2,1,0:T(8,128)(2,1)} %tile_val.1) | copy-start | bytes 3244036
  7.2 56.7 %all-gather.2.cloned.1.call-start = ((), (), s32[]{:S(2)}) async-start(), calls=%async_computation | async-start | bytes 1769472 | tf_op jit(solution)/shard_map/all_gather | solution.py:486
  10.8 0.7 copy-start.1
  11.4 0.7 copy-start.2
  12.1 1.1 copy-start.4
  12.1 1.1 copy-start.6
  13.2 50.7 %copy-start.5 = (bf16[192,1024]{1,0:T(8,128)(2,1)S(1)}, bf16[192,1024]{1,0:T(8,128)(2,1)}, u32[]{:S(2)}) copy-start(bf16[192,1024]{1,0:T(8,128)(2,1)} %cot_ref.1) | copy-start | bytes 1179652
  13.2 50.7 %copy-start.7 = (f32[1024]{0:T(1024)S(1)}, f32[1024]{0:T(1024)}, u32[]{:S(2)}) copy-start(f32[1024]{0:T(1024)} %param.18) | copy-start | bytes 12292
  63.9 1.4 %copy-start.3 = (bf16[1024,768]{1,0:T(8,128)(2,1)S(1)}, bf16[1024,768]{1,0:T(8,128)(2,1)}, u32[]{:S(2)}) copy-start(bf16[1024,768]{1,0:T(8,128)(2,1)} %all-gather.2.cloned.1.call-done.weight_ref) | copy-start | bytes 4718596
Sparse Core Ops, SparseCore 0:
  10.8 53.1 all-gather.1

commit v3 on v2

--- a/solution.py
+++ b/solution.py
@@ -42,7 +42,24 @@
 
 
 def hops_kernel(
-    nodes, send_block, features, scale, matrix, rows, source, outgoing, frame, acc, s_sem, r_sem
+    nodes,
+    send_block,
+    features,
+    scale,
+    matrix,
+    weight,
+    rows,
+    full,
+    source,
+    outgoing,
+    frame,
+    acc,
+    s_sem,
+    r_sem,
+    z_s,
+    z_r,
+    x_s,
+    x_r,
 ):
     node = lax.axis_index("node")
     feat = lax.axis_index("feat")
@@ -60,6 +77,75 @@
     put_source(features[...] * scale[...])
     rows[:, pl.ds(0, panel)] = features[...].astype(jnp.bfloat16)
     pl.semaphore_wait(barrier, nodes - 1)
+
+    units = weight.shape[0]
+    lane, depth = lax.rem(node, 2), node // 2
+    depths = nodes // 2
+    ways = ((0, 2), (1, -2))
+
+    def unit_copy(origin, s, r, device):
+        part = full.at[pl.ds(pl.multiple_of(origin * units, 16), units), :]
+        return pltpu.make_async_remote_copy(
+            src_ref=part,
+            dst_ref=part,
+            send_sem=s,
+            recv_sem=r,
+            device_id=device,
+            device_id_type=MESH,
+        )
+
+    def reaches(way, turn):
+        return depth >= turn if way == 0 else depth + turn < depths
+
+    def goes_on(way):
+        return depth + 1 < depths if way == 0 else depth > 0
+
+    def along(way, shift, turn, start_turn):
+        return unit_copy(
+            node - shift * turn,
+            z_s.at[way, start_turn],
+            z_r.at[way, start_turn],
+            (node + shift, feat),
+        )
+
+    def across(way, shift, turn, origin_lane):
+        return unit_copy(
+            (depth - (shift // 2) * turn) * 2 + origin_lane,
+            x_s.at[way, turn],
+            x_r.at[way, turn],
+            (node + 1 - 2 * lane, feat),
+        )
+
+    def weight_turn(turn):
+        for way, shift in ways:
+
+            @pl.when(reaches(way, turn))
+            def _():
+                if turn > 0:
+                    along(way, shift, turn, turn - 1).wait_recv()
+
+                @pl.when(goes_on(way))
+                def _():
+                    along(way, shift, turn, turn).start()
+
+                if turn > 0 or way == 0:
+                    across(way, shift, turn, lane).start()
+
+    def weight_end():
+        for turn in range(depths):
+            for way, shift in ways:
+
+                @pl.when(reaches(way, turn))
+                def _():
+                    @pl.when(goes_on(way))
+                    def _():
+                        along(way, shift, turn, turn).wait_send()
+
+                    if turn > 0 or way == 0:
+                        across(way, shift, turn, 1 - lane).wait_recv()
+                        across(way, shift, turn, lane).wait_send()
+
+    full[pl.ds(pl.multiple_of(node * units, 16), units), :] = weight[...]
 
     group = min(nodes, 8)
     copies = []
@@ -89,6 +175,8 @@
                     device_id_type=MESH,
                 )
             )
+        if step < depths:
+            weight_turn(step)
         frame[step, node] = jnp.zeros((block, panel), jnp.bfloat16)
         acc[...] = jnp.dot(
             matrix[:, pl.ds(0, own_nodes)],
@@ -119,11 +207,14 @@
         rows[:, pl.ds((step + 1) * panel, panel)] = hop_value.astype(jnp.bfloat16)
         if step + 1 < HOPS:
             put_source(hop_value * scale[...])
+    for turn in range(HOPS, depths):
+        weight_turn(turn)
+    weight_end()
     for copy in copies:
         copy.wait_send()
 
 
-def hops(features, scale, matrix, send_block, block):
+def hops(features, scale, matrix, send_block, weight, block):
     nodes = lax.axis_size("node")
     own_nodes, panel = features.shape
     smem = pl.BlockSpec(memory_space=pltpu.SMEM)
@@ -131,9 +222,12 @@
     dma = pltpu.SemaphoreType.DMA
     return pl.pallas_call(
         functools.partial(hops_kernel, nodes),
-        out_shape=jax.ShapeDtypeStruct((own_nodes, (HOPS + 1) * panel), jnp.bfloat16),
-        in_specs=[smem, vmem, vmem, vmem],
-        out_specs=vmem,
+        out_shape=(
+            jax.ShapeDtypeStruct((own_nodes, (HOPS + 1) * panel), jnp.bfloat16),
+            jax.ShapeDtypeStruct((nodes * weight.shape[0], weight.shape[1]), jnp.bfloat16),
+        ),
+        in_specs=[smem, vmem, vmem, vmem, vmem],
+        out_specs=(vmem, vmem),
         scratch_shapes=[
             pltpu.VMEM((own_nodes // block, block, panel), jnp.bfloat16),
             pltpu.VMEM((HOPS, nodes - 1, block, panel), jnp.bfloat16),
@@ -141,6 +235,10 @@
             pltpu.VMEM((own_nodes, panel), jnp.float32),
             dma((HOPS, nodes - 1)),
             dma((HOPS, nodes - 1)),
+            dma((2, nodes // 2)),
+            dma((2, nodes // 2)),
+            dma((2, nodes // 2)),
+            dma((2, nodes // 2)),
         ],
         compiler_params=pltpu.CompilerParams(
             collective_id=1, has_side_effects=True, vmem_limit_bytes=48 * 1024 * 1024
@@ -151,7 +249,7 @@
             transcendentals=0,
         ),
         name="hops",
-    )(send_block, features, scale, matrix)
+    )(send_block, features, scale, matrix, weight)
 
 
 def layer_kernel(
@@ -483,9 +581,11 @@
     cotangent,
 ):
     row_scale = lax.rsqrt(degrees.astype(jnp.float32))[:, None]
-    flat_weight = lax.all_gather(weight.reshape(weight.shape[0], -1), "node", axis=0, tiled=True)
+    own_weight = weight.reshape(weight.shape[0], -1)
     matrix = dense_matrix(tile_row, tile_col, tile_count, tile_val, features.shape[0])
-    rows = hops(features, row_scale, matrix, send_block, tile_val.shape[-1])
+    rows, flat_weight = hops(
+        features, row_scale, matrix, send_block, own_weight, tile_val.shape[-1]
+    )
     output, weight_grad, bias_grad = layer(rows, flat_weight, out_bias, cotangent)
     return (output, weight_grad.reshape(weight.shape), bias_grad[0])
 

time: 117 us -> 103 us (0.88)
  between operations: 14.7 us -> 1.47 us
  waiting for transfers between devices: 12 us -> 0 us
  Pallas kernels: 81.9 us -> 93.3 us
    pallas_call x1, Pallas kernels: 38.7 us -> 51.1 us  [hops(): pl.pallas_call(functools.partial(hops_kernel, nodes), out_shape=(jax.Shap...]
    all_gather x1 -> x0, waiting for transfers between devices: 12 us -> none  [local(): lax.all_gather(weight.reshape(weight.shape[0], -1), 'node', axis=0, tiled...]
  transfers between devices with their start and end apart: 1 -> 0, of which waited for: 1 -> 0; matrix products, arithmetic and copies ran while one was open for 1% -> 0% of each run, Pallas kernels for 34% -> 0%
where the time goes in v3:
time: 103 us; the launch traced here: 102 us
  Pallas kernels  93.3 us (91%)
  local copies, waits for them, and re-layouts  6.66 us (6%)
  between operations  1.47 us (1%)
    pallas_call x1, Pallas kernels, hops(): pl.pallas_call(functools.partial(hops_kernel, nodes), out_shape=(jax.Shap...  51.1 us
    pallas_call x1, Pallas kernels, layer(): pl.pallas_call(functools.partial(layer_kernel, nodes, feats, cols), out_s...  41.1 us
    unnamed x20, local copies, waits for them, and re-layouts  6.2 us

profile of v3, /device:TPU:0, one launch (start us, length us, event | category | flops | bytes accessed | tf_op | source)
XLA Modules:
  0.0 102.1 jit_solution(7857795029075532466)
XLA Ops:
  0.6 0.0 copy-start.1
  1.4 0.7 convert_rsqrt_fusion
  2.1 1.1 %copy.15 = bf16[128,3,256]{0,2,1:T(8,128)(2,1)S(1)} copy(bf16[128,3,256]{2,0,1:T(8,128)(2,1)} %param.17) | data formatting | bytes 393216 | tf_op args[7]
  3.2 0.2 copy.17.weight
  3.3 0.2 broadcast_in_dim.8.scale
  3.5 0.0 copy-done.1
  3.5 0.0 copy-start.2
  3.5 0.6 copy-done.2
  4.1 0.0 copy-start.3
  4.2 0.7 copy-done.3
  4.8 0.0 copy-start.4
  4.8 1.1 %matrix.1 = bf16[768,1792]{1,0:T(8,128)(2,1)S(1)} custom-call(s32[1,33]{1,0:T(1,128)S(1)} %copy-done.2, s32[1,33]{1,0:T(1,128)S(1)} %copy-done.3, s32[1]{0:T(128)S(6)} %copy.22.tile_count, bf16[1,33,128,128]{3,2,1,0:T(8,128)(2,1)S(1)} %copy-done.1), custom_call_target="tpu_custom_call" | custom-call | tf_op jit(solution)/shard_map/matrix/pallas_call | solution.py:34
  5.9 0.0 copy-start
  6.0 1.5 %copy-done = bf16[768,1792]{1,0:T(8,128)(2,1)} copy-done((bf16[768,1792]{1,0:T(8,128)(2,1)}, bf16[768,1792]{1,0:T(8,128)(2,1)S(1)}, u32[]{:S(2)}) %copy-start) | copy-done | bytes 2752536
  7.5 0.0 copy-done.4
  7.5 0.0 copy-done.6
  7.5 51.1 %hops.1 = (bf16[768,768]{1,0:T(8,128)(2,1)S(1)}, bf16[1024,768]{1,0:T(8,128)(2,1)S(1)}) custom-call(s32[8,8]{1,0:T(8,128)S(1)} %copy-done.6, f32[768,256]{1,0:T(8,128)S(1)} %copy-done.4, f32[768,1]{1,0:T(8,128)S(1)} %broadcast_in_dim.8.scale, bf16[768,1792]{1,0:T(8,128)(2,1)} %copy-done, bf16[128,768]{1,0:T(8,128)(2,1)S(1)} %copy.17.weight), custom_call_target="tpu_custom_call" | custom-call | flops 1409286144 | bytes 104857600 | tf_op jit(solution)/shard_map/hops/pallas_call | solution.py:223
  58.6 0.0 copy-done.5
  58.6 0.0 copy-done.7
  58.6 41.1 %layer.1 = (bf16[192,1024]{1,0:T(8,128)(2,1)S(1)}, f32[128,768]{1,0:T(8,128)S(1)}, f32[1,1024]{1,0:T(1,128)S(1)}) custom-call(bf16[768,768]{1,0:T(8,128)(2,1)S(1)} %get-tuple-element.8.rows_ref, bf16[1024,768]{1,0:T(8,128)(2,1)S(1)} %get-tuple-element.9.weight_ref, f32[1,1024]{1,0:T(1,128)S(1)} %bitcast.5, bf16[192,1024]{1,0:T(8,128)(2,1)S(1)} %copy-done.5), custom_call_target="tpu_custom_call" | custom-call | flops 2415919104 | bytes 6291456 | tf_op jit(solution)/shard_map/layer/pallas_call | solution.py:521
  99.7 0.2 copy.18
  99.9 0.9 copy.19
  100.8 0.7 copy.23
  101.5 0.6 copy.24
  (3 shorter events, 0.0 us)
Async XLA Ops:
  0.6 2.9 %copy-start.1 = (bf16[1,33,128,128]{3,2,1,0:T(8,128)(2,1)S(1)}, bf16[1,33,128,128]{3,2,1,0:T(8,128)(2,1)}, u32[]{:S(2)}) copy-start(bf16[1,33,128,128]{3,2,1,0:T(8,128)(2,1)} %tile_val.1) | copy-start | bytes 3244036
  3.5 0.7 copy-start.2
  4.1 0.7 copy-start.3
  4.8 2.7 %copy-start.4 = (f32[768,256]{1,0:T(8,128)S(1)}, f32[768,256]{1,0:T(8,128)}, u32[]{:S(2)}) copy-start(f32[768,256]{1,0:T(8,128)} %features.1) | copy-start | bytes 2359300
  4.8 2.7 %copy-start.6 = (s32[8,8]{1,0:T(8,128)S(1)}, s32[8,8]{1,0:T(8,128)}, u32[]{:S(2)}) copy-start(s32[8,8]{1,0:T(8,128)} %send_block.1) | copy-start | bytes 772
  5.9 1.5 %copy-start = (bf16[768,1792]{1,0:T(8,128)(2,1)}, bf16[768,1792]{1,0:T(8,128)(2,1)S(1)}, u32[]{:S(2)}) copy-start(bf16[768,1792]{1,0:T(8,128)(2,1)S(1)} %matrix.1) | copy-start | bytes 8257540
  7.5 51.1 %copy-start.5 = (bf16[192,1024]{1,0:T(8,128)(2,1)S(1)}, bf16[192,1024]{1,0:T(8,128)(2,1)}, u32[]{:S(2)}) copy-start(bf16[192,1024]{1,0:T(8,128)(2,1)} %cot_ref.1) | copy-start | bytes 1179652
  7.5 51.1 %copy-start.7 = (f32[1024]{0:T(1024)S(1)}, f32[1024]{0:T(1024)}, u32[]{:S(2)}) copy-start(f32[1024]{0:T(1024)} %param.18) | copy-start | bytes 12292

commit v4 on v3

--- a/solution.py
+++ b/solution.py
@@ -78,7 +78,7 @@
     rows[:, pl.ds(0, panel)] = features[...].astype(jnp.bfloat16)
     pl.semaphore_wait(barrier, nodes - 1)
 
-    units = weight.shape[0]
+    units = weight.shape[1]
     lane, depth = lax.rem(node, 2), node // 2
     depths = nodes // 2
     ways = ((0, 2), (1, -2))
@@ -145,7 +145,10 @@
                         across(way, shift, turn, 1 - lane).wait_recv()
                         across(way, shift, turn, lane).wait_send()
 
-    full[pl.ds(pl.multiple_of(node * units, 16), units), :] = weight[...]
+    for kind in range(weight.shape[0]):
+        full[
+            pl.ds(pl.multiple_of(node * units, 16), units), pl.ds(kind * panel, panel)
+        ] = weight[kind]
 
     group = min(nodes, 8)
     copies = []
@@ -183,6 +186,8 @@
             source[...].reshape(own_nodes, panel),
             preferred_element_type=jnp.float32,
         )
+        if step == HOPS - 1 and HOPS < depths:
+            weight_turn(HOPS)
         for arrival in arrivals:
             arrival.wait_recv()
 
@@ -207,7 +212,7 @@
         rows[:, pl.ds((step + 1) * panel, panel)] = hop_value.astype(jnp.bfloat16)
         if step + 1 < HOPS:
             put_source(hop_value * scale[...])
-    for turn in range(HOPS, depths):
+    for turn in range(HOPS + 1, depths):
         weight_turn(turn)
     weight_end()
     for copy in copies:
@@ -224,7 +229,7 @@
         functools.partial(hops_kernel, nodes),
         out_shape=(
             jax.ShapeDtypeStruct((own_nodes, (HOPS + 1) * panel), jnp.bfloat16),
-            jax.ShapeDtypeStruct((nodes * weight.shape[0], weight.shape[1]), jnp.bfloat16),
+            jax.ShapeDtypeStruct((nodes * weight.shape[1], (HOPS + 1) * panel), jnp.bfloat16),
         ),
         in_specs=[smem, vmem, vmem, vmem, vmem],
         out_specs=(vmem, vmem),
@@ -299,7 +304,7 @@
     highs = feats // 2
     lane, depth = lax.rem(node, 2), node // 2
     own_rows = cot_ref.shape[0]
-    units = wgrad_ref.shape[0]
+    units = wgrad_ref.shape[1]
     pieces = weight_ref.shape[0] // cols
     share = cols // (2 * units)
     pair = (node, feat + 1 - 2 * side)
@@ -465,7 +470,7 @@
             x_copies[slot].wait()
             total = x_held[slot] + x_recv[slot].astype(jnp.float32)
             if slot == pieces * share - 1:
-                wgrad_ref[...] = total
+                x_held[slot] = total
                 continue
             z_send[slot] = total.astype(jnp.bfloat16)
             copy = remote(
@@ -498,9 +503,13 @@
         bias_total = bias_total + bias_all[part]
     bgrad_ref[...] = bias_total
 
+    last = pieces * share - 1
     for slot, copy in enumerate(z_copies):
         copy.wait()
-        wgrad_ref[...] += z_recv[slot].astype(jnp.float32)
+        x_held[last] += z_recv[slot].astype(jnp.float32)
+    panel = wgrad_ref.shape[2]
+    for kind in range(wgrad_ref.shape[0]):
+        wgrad_ref[kind] = x_held[last, :, pl.ds(kind * panel, panel)]
     for copy in started:
         copy.wait_send()
 
@@ -522,7 +531,7 @@
         functools.partial(layer_kernel, nodes, feats, cols),
         out_shape=(
             jax.ShapeDtypeStruct((own_rows, outs), jnp.bfloat16),
-            jax.ShapeDtypeStruct((units, width), jnp.float32),
+            jax.ShapeDtypeStruct((HOPS + 1, units, width // (HOPS + 1)), jnp.float32),
             jax.ShapeDtypeStruct((1, outs), jnp.float32),
         ),
         in_specs=[vmem] * 4,
@@ -581,13 +590,13 @@
     cotangent,
 ):
     row_scale = lax.rsqrt(degrees.astype(jnp.float32))[:, None]
-    own_weight = weight.reshape(weight.shape[0], -1)
+    own_weight = weight.transpose(1, 0, 2)
     matrix = dense_matrix(tile_row, tile_col, tile_count, tile_val, features.shape[0])
     rows, flat_weight = hops(
         features, row_scale, matrix, send_block, own_weight, tile_val.shape[-1]
     )
     output, weight_grad, bias_grad = layer(rows, flat_weight, out_bias, cotangent)
-    return (output, weight_grad.reshape(weight.shape), bias_grad[0])
+    return (output, weight_grad.transpose(1, 0, 2), bias_grad[0])
 
 
 def solution(mesh):

time: 103 us -> 102 us (level)
    unnamed x20 -> x21, local copies, waits for them, and re-layouts: 6.2 us -> 6.19 us
where the time goes in v4:
time: 102 us
  Pallas kernels  93.3 us (91%)
  local copies, waits for them, and re-layouts  6.35 us (6%)
  between operations  1.36 us (1%)
    pallas_call x1, Pallas kernels, hops(): pl.pallas_call(functools.partial(hops_kernel, nodes), out_shape=(jax.Shap...  51.2 us
    pallas_call x1, Pallas kernels, layer(): pl.pallas_call(functools.partial(layer_kernel, nodes, feats, cols), out_s...  41.1 us
    unnamed x21, local copies, waits for them, and re-layouts  6.19 us

profile of v4, /device:TPU:0, one launch (start us, length us, event | category | flops | bytes accessed | tf_op | source)
XLA Modules:
  0.0 101.7 jit_solution(12969468846864136463)
XLA Ops:
  1.3 0.7 convert_rsqrt_fusion
  2.0 0.2 broadcast_in_dim.8.scale
  2.1 0.0 copy-start.1
  2.1 1.2 %copy-done.1 = bf16[1,33,128,128]{3,2,1,0:T(8,128)(2,1)S(1)} copy-done((bf16[1,33,128,128]{3,2,1,0:T(8,128)(2,1)S(1)}, bf16[1,33,128,128]{3,2,1,0:T(8,128)(2,1)}, u32[]{:S(2)}) %copy-start.1) | copy-done | bytes 1081368
  3.4 0.0 copy-start.2
  3.4 0.7 copy-done.2
  4.0 0.0 copy-start.3
  4.0 0.7 copy-done.3
  4.7 0.0 copy-start.4
  4.7 0.0 copy-start.6
  4.7 1.0 %matrix.1 = bf16[768,1792]{1,0:T(8,128)(2,1)S(1)} custom-call(s32[1,33]{1,0:T(1,128)S(1)} %copy-done.2, s32[1,33]{1,0:T(1,128)S(1)} %copy-done.3, s32[1]{0:T(128)S(6)} %copy.17.tile_count, bf16[1,33,128,128]{3,2,1,0:T(8,128)(2,1)S(1)} %copy-done.1), custom_call_target="tpu_custom_call" | custom-call | tf_op jit(solution)/shard_map/matrix/pallas_call | solution.py:34
  5.7 0.0 copy-start
  5.8 1.5 %copy-done = bf16[768,1792]{1,0:T(8,128)(2,1)} copy-done((bf16[768,1792]{1,0:T(8,128)(2,1)}, bf16[768,1792]{1,0:T(8,128)(2,1)S(1)}, u32[]{:S(2)}) %copy-start) | copy-done | bytes 2752536
  7.3 0.0 copy-done.4
  7.3 0.0 copy-done.6
  7.3 0.0 copy-done.7
  7.3 0.0 copy-start.8
  7.3 51.2 %hops.1 = (bf16[768,768]{1,0:T(8,128)(2,1)S(1)}, bf16[1024,768]{1,0:T(8,128)(2,1)S(1)}) custom-call(s32[8,8]{1,0:T(8,128)S(1)} %copy-done.7, f32[768,256]{1,0:T(8,128)S(1)} %copy-done.4, f32[768,1]{1,0:T(8,128)S(1)} %broadcast_in_dim.8.scale, bf16[768,1792]{1,0:T(8,128)(2,1)} %copy-done, bf16[3,128,256]{2,1,0:T(8,128)(2,1)S(1)} %bitcast.6), custom_call_target="tpu_custom_call" | custom-call | flops 1409286144 | bytes 104857600 | tf_op jit(solution)/shard_map/hops/pallas_call | solution.py:228
  58.5 0.0 copy-done.5
  58.6 0.0 copy-done.8
  58.6 41.1 %layer.1 = (bf16[192,1024]{1,0:T(8,128)(2,1)S(1)}, f32[3,128,256]{2,1,0:T(8,128)S(1)}, f32[1,1024]{1,0:T(1,128)S(1)}) custom-call(bf16[768,768]{1,0:T(8,128)(2,1)S(1)} %get-tuple-element.8.rows_ref, bf16[1024,768]{1,0:T(8,128)(2,1)S(1)} %get-tuple-element.9.weight_ref, f32[1,1024]{1,0:T(1,128)S(1)} %bitcast.7, bf16[192,1024]{1,0:T(8,128)(2,1)S(1)} %copy-done.5), custom_call_target="tpu_custom_call" | custom-call | flops 2415919104 | bytes 6291456 | tf_op jit(solution)/shard_map/layer/pallas_call | solution.py:530
  99.6 0.7 copy.18
  100.4 0.7 copy.19
  101.1 0.6 copy.20
  (2 shorter events, 0.0 us)
Async XLA Ops:
  2.1 1.2 %copy-start.1 = (bf16[1,33,128,128]{3,2,1,0:T(8,128)(2,1)S(1)}, bf16[1,33,128,128]{3,2,1,0:T(8,128)(2,1)}, u32[]{:S(2)}) copy-start(bf16[1,33,128,128]{3,2,1,0:T(8,128)(2,1)} %tile_val.1) | copy-start | bytes 3244036
  3.4 0.7 copy-start.2
  4.0 0.7 copy-start.3
  4.7 2.6 %copy-start.4 = (f32[768,256]{1,0:T(8,128)S(1)}, f32[768,256]{1,0:T(8,128)}, u32[]{:S(2)}) copy-start(f32[768,256]{1,0:T(8,128)} %features.1) | copy-start | bytes 2359300
  4.7 2.6 %copy-start.6 = (bf16[128,3,256]{2,0,1:T(8,128)(2,1)S(1)}, bf16[128,3,256]{2,0,1:T(8,128)(2,1)}, u32[]{:S(2)}) copy-start(bf16[128,3,256]{2,0,1:T(8,128)(2,1)} %param.17) | copy-start | bytes 589828
  4.7 2.6 %copy-start.7 = (s32[8,8]{1,0:T(8,128)S(1)}, s32[8,8]{1,0:T(8,128)}, u32[]{:S(2)}) copy-start(s32[8,8]{1,0:T(8,128)} %send_block.1) | copy-start | bytes 772
  5.7 1.5 %copy-start = (bf16[768,1792]{1,0:T(8,128)(2,1)}, bf16[768,1792]{1,0:T(8,128)(2,1)S(1)}, u32[]{:S(2)}) copy-start(bf16[768,1792]{1,0:T(8,128)(2,1)S(1)} %matrix.1) | copy-start | bytes 8257540
  7.3 51.3 %copy-start.5 = (bf16[192,1024]{1,0:T(8,128)(2,1)S(1)}, bf16[192,1024]{1,0:T(8,128)(2,1)}, u32[]{:S(2)}) copy-start(bf16[192,1024]{1,0:T(8,128)(2,1)} %cot_ref.1) | copy-start | bytes 1179652
  7.3 51.3 %copy-start.8 = (f32[1024]{0:T(1024)S(1)}, f32[1024]{0:T(1024)}, u32[]{:S(2)}) copy-start(f32[1024]{0:T(1024)} %param.18) | copy-start | bytes 12292

commit v5 on v4

--- a/solution.py
+++ b/solution.py
@@ -178,16 +178,16 @@
                     device_id_type=MESH,
                 )
             )
-        if step < depths:
-            weight_turn(step)
+        if 2 * step < depths:
+            weight_turn(2 * step)
         frame[step, node] = jnp.zeros((block, panel), jnp.bfloat16)
         acc[...] = jnp.dot(
             matrix[:, pl.ds(0, own_nodes)],
             source[...].reshape(own_nodes, panel),
             preferred_element_type=jnp.float32,
         )
-        if step == HOPS - 1 and HOPS < depths:
-            weight_turn(HOPS)
+        if 2 * step + 1 < depths:
+            weight_turn(2 * step + 1)
         for arrival in arrivals:
             arrival.wait_recv()
 
@@ -212,7 +212,7 @@
         rows[:, pl.ds((step + 1) * panel, panel)] = hop_value.astype(jnp.bfloat16)
         if step + 1 < HOPS:
             put_source(hop_value * scale[...])
-    for turn in range(HOPS + 1, depths):
+    for turn in range(2 * HOPS, depths):
         weight_turn(turn)
     weight_end()
     for copy in copies:

time: 102 us -> 102 us (level)
    pallas_call x1, Pallas kernels: 51.2 us -> 50.1 us  [hops(): pl.pallas_call(functools.partial(hops_kernel, nodes), out_shape=(jax.Shap...]
where the time goes in v5:
time: 102 us
  Pallas kernels  93.2 us (91%)
  local copies, waits for them, and re-layouts  6.35 us (6%)
  between operations  1.36 us (1%)
    pallas_call x1, Pallas kernels, hops(): pl.pallas_call(functools.partial(hops_kernel, nodes), out_shape=(jax.Shap...  50.1 us
    pallas_call x1, Pallas kernels, layer(): pl.pallas_call(functools.partial(layer_kernel, nodes, feats, cols), out_s...  42 us
    unnamed x21, local copies, waits for them, and re-layouts  6.19 us

profile of v5, /device:TPU:0, one launch (start us, length us, event | category | flops | bytes accessed | tf_op | source)
XLA Modules:
  0.0 101.6 jit_solution(9404450964728363519)
XLA Ops:
  1.3 0.7 convert_rsqrt_fusion
  2.0 0.2 broadcast_in_dim.8.scale
  2.1 0.0 copy-start.1
  2.1 1.2 %copy-done.1 = bf16[1,33,128,128]{3,2,1,0:T(8,128)(2,1)S(1)} copy-done((bf16[1,33,128,128]{3,2,1,0:T(8,128)(2,1)S(1)}, bf16[1,33,128,128]{3,2,1,0:T(8,128)(2,1)}, u32[]{:S(2)}) %copy-start.1) | copy-done | bytes 1081368
  3.4 0.0 copy-start.2
  3.4 0.7 copy-done.2
  4.0 0.0 copy-start.3
  4.0 0.7 copy-done.3
  4.7 0.0 copy-start.4
  4.7 0.0 copy-start.6
  4.7 1.1 %matrix.1 = bf16[768,1792]{1,0:T(8,128)(2,1)S(1)} custom-call(s32[1,33]{1,0:T(1,128)S(1)} %copy-done.2, s32[1,33]{1,0:T(1,128)S(1)} %copy-done.3, s32[1]{0:T(128)S(6)} %copy.17.tile_count, bf16[1,33,128,128]{3,2,1,0:T(8,128)(2,1)S(1)} %copy-done.1), custom_call_target="tpu_custom_call" | custom-call | tf_op jit(solution)/shard_map/matrix/pallas_call | solution.py:34
  5.8 0.0 copy-start
  5.8 1.5 %copy-done = bf16[768,1792]{1,0:T(8,128)(2,1)} copy-done((bf16[768,1792]{1,0:T(8,128)(2,1)}, bf16[768,1792]{1,0:T(8,128)(2,1)S(1)}, u32[]{:S(2)}) %copy-start) | copy-done | bytes 2752536
  7.3 0.0 copy-done.4
  7.3 0.0 copy-done.6
  7.3 0.0 copy-done.7
  7.3 0.0 copy-start.8
  7.3 50.1 %hops.1 = (bf16[768,768]{1,0:T(8,128)(2,1)S(1)}, bf16[1024,768]{1,0:T(8,128)(2,1)S(1)}) custom-call(s32[8,8]{1,0:T(8,128)S(1)} %copy-done.7, f32[768,256]{1,0:T(8,128)S(1)} %copy-done.4, f32[768,1]{1,0:T(8,128)S(1)} %broadcast_in_dim.8.scale, bf16[768,1792]{1,0:T(8,128)(2,1)} %copy-done, bf16[3,128,256]{2,1,0:T(8,128)(2,1)S(1)} %bitcast.6), custom_call_target="tpu_custom_call" | custom-call | flops 1409286144 | bytes 104857600 | tf_op jit(solution)/shard_map/hops/pallas_call | solution.py:228
  57.5 0.0 copy-done.5
  57.5 0.0 copy-done.8
  57.5 42.0 %layer.1 = (bf16[192,1024]{1,0:T(8,128)(2,1)S(1)}, f32[3,128,256]{2,1,0:T(8,128)S(1)}, f32[1,1024]{1,0:T(1,128)S(1)}) custom-call(bf16[768,768]{1,0:T(8,128)(2,1)S(1)} %get-tuple-element.8.rows_ref, bf16[1024,768]{1,0:T(8,128)(2,1)S(1)} %get-tuple-element.9.weight_ref, f32[1,1024]{1,0:T(1,128)S(1)} %bitcast.7, bf16[192,1024]{1,0:T(8,128)(2,1)S(1)} %copy-done.5), custom_call_target="tpu_custom_call" | custom-call | flops 2415919104 | bytes 6291456 | tf_op jit(solution)/shard_map/layer/pallas_call | solution.py:530
  99.5 0.7 copy.18
  100.3 0.7 copy.19
  101.0 0.6 copy.20
  (2 shorter events, 0.0 us)
Async XLA Ops:
  2.1 1.2 %copy-start.1 = (bf16[1,33,128,128]{3,2,1,0:T(8,128)(2,1)S(1)}, bf16[1,33,128,128]{3,2,1,0:T(8,128)(2,1)}, u32[]{:S(2)}) copy-start(bf16[1,33,128,128]{3,2,1,0:T(8,128)(2,1)} %tile_val.1) | copy-start | bytes 3244036
  3.4 0.7 copy-start.2
  4.0 0.7 copy-start.3
  4.7 2.6 %copy-start.4 = (f32[768,256]{1,0:T(8,128)S(1)}, f32[768,256]{1,0:T(8,128)}, u32[]{:S(2)}) copy-start(f32[768,256]{1,0:T(8,128)} %features.1) | copy-start | bytes 2359300
  4.7 2.6 %copy-start.6 = (bf16[128,3,256]{2,0,1:T(8,128)(2,1)S(1)}, bf16[128,3,256]{2,0,1:T(8,128)(2,1)}, u32[]{:S(2)}) copy-start(bf16[128,3,256]{2,0,1:T(8,128)(2,1)} %param.17) | copy-start | bytes 589828
  4.7 2.6 %copy-start.7 = (s32[8,8]{1,0:T(8,128)S(1)}, s32[8,8]{1,0:T(8,128)}, u32[]{:S(2)}) copy-start(s32[8,8]{1,0:T(8,128)} %send_block.1) | copy-start | bytes 772
  5.8 1.5 %copy-start = (bf16[768,1792]{1,0:T(8,128)(2,1)}, bf16[768,1792]{1,0:T(8,128)(2,1)S(1)}, u32[]{:S(2)}) copy-start(bf16[768,1792]{1,0:T(8,128)(2,1)S(1)} %matrix.1) | copy-start | bytes 8257540
  7.3 50.1 %copy-start.5 = (bf16[192,1024]{1,0:T(8,128)(2,1)S(1)}, bf16[192,1024]{1,0:T(8,128)(2,1)}, u32[]{:S(2)}) copy-start(bf16[192,1024]{1,0:T(8,128)(2,1)} %cot_ref.1) | copy-start | bytes 1179652
  7.3 50.1 %copy-start.8 = (f32[1024]{0:T(1024)S(1)}, f32[1024]{0:T(1024)}, u32[]{:S(2)}) copy-start(f32[1024]{0:T(1024)} %param.18) | copy-start | bytes 12292
